TPU v7x, 256 devices: a whole 4x4x8 slice. The times are simulated.
256 devices in a mesh: head: 4 (over y_hi, core), blk: 64 (over x, z, y_lo).
Axes of the slice: x: 4, y: 4 (y_hi: 2, y_lo: 2; y = y_hi * 2 + y_lo), z: 8, core: 2. Of those that a mesh axis runs over, the one named last changes fastest.
Arguments:
- queries: bfloat16 [16384, 512], P(('blk', 'head')), may hold values from -6 to 6
- keys: bfloat16 [16384, 512], P(('blk', 'head')), may hold values from -6 to 6
- values: bfloat16 [16384, 512], P(('blk', 'head')), may hold values from -6 to 6
- upstream: bfloat16 [16384, 512], P(('blk', 'head')), may hold values from -6 to 6
Outputs:
- attended: bfloat16 [16384, 512], P(('blk', 'head'))
- query_grad: bfloat16 [16384, 512], P(('blk', 'head'))
- key_grad: bfloat16 [16384, 512], P(('blk', 'head'))
- value_grad: bfloat16 [16384, 512], P(('blk', 'head'))
All inputs are finite; a program needn't handle non-finite values.
Results may differ from a plain program's by a relative error of at most 0.02.
Values may be sent and summed in bfloat16 or wider, within the bound.
No kernel may reach another device: no remote copies, remote signals or barrier semaphores. Data moves between devices by JAX's collectives and lax.ppermute only.
A program may use at most 64 MiB of HBM per device.

v0:
```python
import math

import jax
import jax.numpy as jnp
from jax import lax
from jax.sharding import PartitionSpec as P

DH = 128


def shifted(x, axis, by):
    devices = lax.axis_size(axis)
    return lax.ppermute(x, axis, [(i, (i + by) % devices) for i in range(devices)])


def shards(queries, keys, values, upstream):
    queries_here, keys_here, values_here, upstream_here = (
        lax.all_to_all(queries, "head", split_axis=1, concat_axis=0, tiled=True),
        lax.all_to_all(keys, "head", split_axis=1, concat_axis=0, tiled=True),
        lax.all_to_all(values, "head", split_axis=1, concat_axis=0, tiled=True),
        lax.all_to_all(upstream, "head", split_axis=1, concat_axis=0, tiled=True),
    )
    row_count = queries_here.shape[0]
    feature_count = queries_here.shape[1]
    head_count = feature_count // DH
    cycle_size = lax.axis_size("blk")
    key_count = row_count * cycle_size
    scaling = 1.0 / math.sqrt(DH)
    query_heads = queries_here.reshape(row_count, head_count, DH)
    upstream_heads = upstream_here.reshape(row_count, head_count, DH)

    def score_block(key_block):
        return (
            jnp.einsum("qhd,khd->hqk", query_heads, key_block, preferred_element_type=jnp.float32)
            * scaling
        )

    running_max = jnp.full((head_count, row_count), -jnp.inf, jnp.float32)
    running_sum = jnp.zeros((head_count, row_count), jnp.float32)
    piece_keys = lax.all_gather(keys_here, "blk", axis=0, tiled=True)
    piece_values = lax.all_gather(values_here, "blk", axis=0, tiled=True)
    piece_rows = piece_keys.shape[0]
    absorb_group_size = math.gcd(piece_rows, 512)
    split_keys = piece_keys.reshape(
        piece_rows // absorb_group_size, absorb_group_size, head_count, DH
    )

    def scan_step(state, key_block):
        old_max, old_sum = state
        scores = score_block(key_block)
        new_max = jnp.maximum(old_max, jnp.max(scores, axis=2))
        new_sum = old_sum * jnp.exp(old_max - new_max) + jnp.sum(
            jnp.exp(scores - new_max[:, :, None]), axis=2
        )
        return ((new_max, new_sum), None)

    (running_max, running_sum), unused = lax.scan(scan_step, (running_max, running_sum), split_keys)
    running_max, running_sum, store_keys, store_values = (
        running_max,
        running_sum,
        piece_keys,
        piece_values,
    )
    log_total = running_max + jnp.log(running_sum)

    def key_slab(store, first, size):
        return lax.dynamic_slice_in_dim(store, first, size, 0).reshape(size, head_count, DH)

    group_size = math.gcd(key_count, 512)
    group_count = key_count // group_size

    def output_turn(turn_index, output_sum):
        key_block = key_slab(store_keys, turn_index * group_size, group_size)
        value_block = key_slab(store_values, turn_index * group_size, group_size)
        weights_low = jnp.exp(score_block(key_block) - log_total[:, :, None]).astype(jnp.bfloat16)
        return output_sum + jnp.einsum(
            "hqk,khd->qhd", weights_low, value_block, preferred_element_type=jnp.float32
        )

    output_sum = lax.fori_loop(
        0, group_count, output_turn, jnp.zeros((row_count, head_count, DH), jnp.float32)
    )
    attended_heads = output_sum.astype(jnp.bfloat16)
    delta = jnp.sum(
        upstream_heads.astype(jnp.float32) * attended_heads.astype(jnp.float32), axis=2
    ).T

    def block_terms(key_block, value_block):
        weights = jnp.exp(score_block(key_block) - log_total[:, :, None])
        weights_low = weights.astype(jnp.bfloat16)
        upstream_dot = jnp.einsum(
            "qhd,khd->hqk", upstream_heads, value_block, preferred_element_type=jnp.float32
        )
        score_grad = (weights * (upstream_dot - delta[:, :, None])).astype(jnp.bfloat16)
        query_term = jnp.einsum(
            "hqk,khd->qhd", score_grad, key_block, preferred_element_type=jnp.float32
        )
        key_term = jnp.einsum(
            "hqk,qhd->khd", score_grad, query_heads, preferred_element_type=jnp.float32
        )
        value_term = jnp.einsum(
            "hqk,qhd->khd", weights_low, upstream_heads, preferred_element_type=jnp.float32
        )
        block_rows = key_block.shape[0]
        return (
            query_term,
            key_term.reshape(block_rows, feature_count),
            value_term.reshape(block_rows, feature_count),
        )

    query_zero = jnp.zeros((row_count, head_count, DH), jnp.float32)
    my_index = lax.axis_index("blk")

    def cycle_turn(turn_index, carried):
        query_sum, key_sum, value_sum = carried
        source_index = (my_index - turn_index) % cycle_size
        key_block = key_slab(store_keys, source_index * row_count, row_count)
        value_block = key_slab(store_values, source_index * row_count, row_count)
        query_term, key_term, value_term = block_terms(key_block, value_block)
        key_sum, value_sum = shifted((key_sum + key_term, value_sum + value_term), "blk", 1)
        return (query_sum + query_term, key_sum, value_sum)

    grad_zero = jnp.zeros((row_count, feature_count), jnp.float32)
    query_sum, key_sum, value_sum = lax.fori_loop(
        0, cycle_size, cycle_turn, (query_zero, grad_zero, grad_zero)
    )
    attended_rows = attended_heads.reshape(row_count, feature_count)
    query_grad = (query_sum * scaling).astype(jnp.bfloat16).reshape(row_count, feature_count)
    key_grad = (key_sum * scaling).astype(jnp.bfloat16)
    value_grad = value_sum.astype(jnp.bfloat16)
    return (
        lax.all_to_all(attended_rows, "head", split_axis=0, concat_axis=1, tiled=True),
        lax.all_to_all(query_grad, "head", split_axis=0, concat_axis=1, tiled=True),
        lax.all_to_all(key_grad, "head", split_axis=0, concat_axis=1, tiled=True),
        lax.all_to_all(value_grad, "head", split_axis=0, concat_axis=1, tiled=True),
    )


def solution(mesh):
    return jax.shard_map(
        shards,
        mesh=mesh,
        in_specs=(
            P(("blk", "head"), None),
            P(("blk", "head"), None),
            P(("blk", "head"), None),
            P(("blk", "head"), None),
        ),
        out_specs=(
            P(("blk", "head"), None),
            P(("blk", "head"), None),
            P(("blk", "head"), None),
            P(("blk", "head"), None),
        ),
        check_vma=False,
    )
```

profile of v0, /device:TPU:1, one launch (start us, length us, event | category | flops | bytes accessed | tf_op | source)
XLA Modules:
  0.0 1585.3 jit_solution(2593250385674905487)
XLA Ops:
  8.0 11.0 all_to_all.146
  42.7 237.4 %all-gather.5.cloned.1.call-done = bf16[16384,128]{1,0:T(8,128)(2,1)} async-done(((bf16[256,128]{1,0:T(8,128)(2,1)}), bf16[16384,128]{1,0:T(8,128)(2,1)}) %all-gather.5.cloned.1.call-update) | async-done | bytes 4194320 | tf_op jit(solution)/shard_map/all_gather | solution.py:40
  280.1 43.2 %while.47 = (s32[]{:T(128)}, f32[1,256]{1,0:T(1,128)S(1)}, f32[1,256]{1,0:T(1,128)S(1)}, bf16[32,512,1,128]{3,1,2,0:T(8,128)(2,1)}, bf16[256,1,128]{2,0,1:T(8,128)(2,1)S(1)}, /*index=5*/s32[]{:T(128)}, s32[]{:T(128)}) while((s32[]{:T(128)}, f32[1,256]{1,0:T(1,128)S(1)}, f32[1,256]{1,0:T(1,128)S(1)}, ...), condition=%wide.region_3.4_spmd.clone, body=%wide.region_0.3_spmd.clone.sunk | while | flops 34080000 | bytes 1258596 | solution.py:57
  323.4 260.5 %all-gather.3.cloned.1.call-done = bf16[16384,128]{1,0:T(8,128)(2,1)} async-done(((bf16[256,128]{1,0:T(8,128)(2,1)}), bf16[16384,128]{1,0:T(8,128)(2,1)}) %all-gather.3.cloned.1.call-update) | async-done | bytes 4194320 | tf_op jit(solution)/shard_map/all_gather | solution.py:41
  583.9 46.9 %while.48 = (s32[]{:T(128)}, f32[256,1,128]{0,2,1:T(8,128)S(1)}, bf16[16384,128]{1,0:T(8,128)(2,1)}, bf16[16384,128]{1,0:T(8,128)(2,1)}, bf16[256,1,128]{2,0,1:T...) while((s32[]{:T(128)}, f32[256,1,128]{0,2,1:T(8,128)S(1)}, ...), condition=%wide.region_5.6_spmd.clone, body=%wide.region_4.5_spmd.clone.sunk | while | flops 67567624 | bytes 592548 | solution.py:80
  632.5 797.1 %while.49 = (s32[]{:T(128)}, f32[256,1,128]{0,2,1:T(8,128)S(1)}, f32[256,128]{1,0:T(8,128)S(1)}, f32[256,128]{1,0:T(8,128)S(1)}, s32[]{:T(128)}, /*index=5*/bf16...) while((s32[]{:T(128)}, f32[256,1,128]{0,2,1:T(8,128)S(1)}, ...), condition=%wide.region_8.9_spmd.clone, body=%wide.region_7.8_spmd.clone.sunk | while | flops 84410384 | bytes 3475882 | solution.py:124
  695.1 7.6 collective-permute-done
  707.8 8.3 collective-permute-done
  721.7 8.1 collective-permute-done
  736.2 7.2 collective-permute-done
  762.7 6.7 collective-permute-done
  774.5 6.7 collective-permute-done
  786.3 6.7 collective-permute-done
  798.0 6.7 collective-permute-done
  809.8 6.7 collective-permute-done
  821.6 6.7 collective-permute-done
  833.4 6.7 collective-permute-done
  845.2 7.6 collective-permute-done
  857.8 8.4 collective-permute-done
  871.6 8.1 collective-permute-done
  886.1 7.2 collective-permute-done
  912.6 6.7 collective-permute-done
  924.4 6.7 collective-permute-done
  936.2 6.7 collective-permute-done
  948.0 6.7 collective-permute-done
  959.7 6.7 collective-permute-done
  971.5 6.7 collective-permute-done
  983.3 6.7 collective-permute-done
  995.1 7.6 collective-permute-done
  1007.7 8.4 collective-permute-done
  1021.5 8.1 collective-permute-done
  1036.1 7.2 collective-permute-done
  1049.9 6.7 collective-permute-done
  1062.7 6.7 collective-permute-done
  1074.4 6.7 collective-permute-done
  1086.2 6.7 collective-permute-done
  1098.0 6.7 collective-permute-done
  1109.8 6.7 collective-permute-done
  1121.6 6.7 collective-permute-done
  1133.3 6.7 collective-permute-done
  1145.1 7.5 collective-permute-done
  1157.8 8.4 collective-permute-done
  1171.5 8.1 collective-permute-done
  1186.1 7.2 collective-permute-done
  1199.9 6.7 collective-permute-done
  1212.7 6.7 collective-permute-done
  1224.5 6.7 collective-permute-done
  1236.2 6.7 collective-permute-done
  1248.0 6.7 collective-permute-done
  1259.8 6.7 collective-permute-done
  1271.6 6.7 collective-permute-done
  1283.4 6.7 collective-permute-done
  1295.1 7.5 collective-permute-done
  1307.8 8.4 collective-permute-done
  1321.4 8.1 collective-permute-done
  1336.1 7.2 collective-permute-done
  1349.8 6.7 collective-permute-done
  1362.6 6.7 collective-permute-done
  1374.4 6.7 collective-permute-done
  1386.2 6.7 collective-permute-done
  1398.0 6.7 collective-permute-done
  1409.7 6.7 collective-permute-done
  1421.5 6.7 collective-permute-done
  1430.2 116.1 %all-to-all-start.7 = ((bf16[4,64,128]{2,1,0:T(8,128)(2,1)}), bf16[4,64,128]{2,1,0:T(8,128)(2,1)S(1)}, u32[]{:S(2)}, u32[]{:S(2)}) async-start(bf16[4,64,128]{2,1,0:T(8,128)(2,1)} %bitcast.19), calls=%async_computation.7 | async-start | bytes 131072 | tf_op jit(solution)/shard_map/all_to_all | solution.py:135
  (753 shorter events, 537.0 us)
Async XLA Ops:
  7.2 273.0 %all-gather.5.cloned.1.call-start = ((), (), s32[]{:S(2)}) async-start(), calls=%async_computation.9 | async-start | bytes 4259840 | tf_op jit(solution)/shard_map/all_gather | solution.py:40
  33.6 550.3 %all-gather.3.cloned.1.call-start = ((), (), s32[]{:S(2)}) async-start(), calls=%async_computation.8 | async-start | bytes 4259840 | tf_op jit(solution)/shard_map/all_gather | solution.py:41
  38.6 592.9 %all-to-all-start.4 = ((bf16[64,4,128]{2,0,1:T(8,128)(2,1)}), bf16[64,4,128]{2,0,1:T(8,128)(2,1)S(1)}, u32[]{:S(2)}, u32[]{:S(2)}) async-start(bf16[64,4,128]{2,0,1:T(8,128)(2,1)} %copy_bitcast_fusion.4), calls=%async_computation.4 | async-start | bytes 131072 | tf_op jit(solution)/shard_map/all_to_all | solution.py:21
  635.0 9.2 collective-permute-start.1
  646.8 9.2 collective-permute-start.1
  658.6 9.2 collective-permute-start.1
  670.4 9.2 collective-permute-start.1
  682.2 9.2 collective-permute-start.1
  693.9 10.2 collective-permute-start.1
  706.4 9.8 collective-permute-start
  706.7 11.3 collective-permute-start.1
  720.2 9.5 collective-permute-start
  720.5 12.0 collective-permute-start.1
  735.1 11.2 collective-permute-start.1
  748.8 10.2 collective-permute-start.1
  761.5 9.2 collective-permute-start.1
  773.3 9.2 collective-permute-start.1
  785.1 9.2 collective-permute-start.1
  796.9 9.2 collective-permute-start.1
  808.6 9.2 collective-permute-start.1
  820.4 9.2 collective-permute-start.1
  832.2 9.2 collective-permute-start.1
  844.0 10.1 collective-permute-start.1
  856.4 9.8 collective-permute-start
  856.7 11.2 collective-permute-start.1
  870.1 9.5 collective-permute-start
  870.4 12.0 collective-permute-start.1
  885.0 11.2 collective-permute-start.1
  898.7 10.2 collective-permute-start.1
  911.5 9.3 collective-permute-start.1
  923.2 9.2 collective-permute-start.1
  935.0 9.2 collective-permute-start.1
  946.8 9.2 collective-permute-start.1
  958.6 9.2 collective-permute-start.1
  970.4 9.2 collective-permute-start.1
  982.1 9.2 collective-permute-start.1
  993.9 10.1 collective-permute-start.1
  1006.3 9.8 collective-permute-start
  1006.6 11.2 collective-permute-start.1
  1020.0 9.6 collective-permute-start
  1020.3 12.1 collective-permute-start.1
  1035.0 11.2 collective-permute-start.1
  1048.7 10.3 collective-permute-start.1
  1061.5 9.3 collective-permute-start.1
  1073.3 9.2 collective-permute-start.1
  1085.1 9.2 collective-permute-start.1
  1096.8 9.2 collective-permute-start.1
  1108.6 9.2 collective-permute-start.1
  1132.2 9.2 collective-permute-start.1
  1144.0 10.1 collective-permute-start.1
  1156.3 9.8 collective-permute-start
  1156.6 11.2 collective-permute-start.1
  1170.1 9.6 collective-permute-start
  1170.3 12.1 collective-permute-start.1
  1185.0 11.2 collective-permute-start.1
  1198.7 10.3 collective-permute-start.1
  1294.0 10.1 collective-permute-start.1
  1306.3 9.8 collective-permute-start
  1306.6 11.2 collective-permute-start.1
  1320.0 9.5 collective-permute-start
  1320.3 12.1 collective-permute-start.1
  1334.9 11.2 collective-permute-start.1
  1348.6 10.3 collective-permute-start.1
  1430.2 120.9 %all-to-all-start.7 = ((bf16[4,64,128]{2,1,0:T(8,128)(2,1)}), bf16[4,64,128]{2,1,0:T(8,128)(2,1)S(1)}, u32[]{:S(2)}, u32[]{:S(2)}) async-start(bf16[4,64,128]{2,1,0:T(8,128)(2,1)} %bitcast.19), calls=%async_computation.7 | async-start | bytes 131072 | tf_op jit(solution)/shard_map/all_to_all | solution.py:135
  (75 other events, 625.9 us)
Sparse Core Ops, SparseCore 0:
  19.2 260.8 all-gather.4
  282.5 301.3 all-gather.2
where the time goes:
time: 1600 us; the launch traced here: 1590 us
  waiting for transfers between devices  1080 us (68%)
  matrix products  306 us (19%)
  starting transfers between devices  152 us (10%)
    ppermute x128, waiting for transfers between devices, shifted(): lax.ppermute(x, axis, [(i, (i + by) % devices) for i in range(devices)])  560 us
    all_gather x1, waiting for transfers between devices, shards(): piece_values = lax.all_gather(values_here, 'blk', axis=0, tiled=True)  260 us
    all_gather x1, waiting for transfers between devices, shards(): piece_keys = lax.all_gather(keys_here, 'blk', axis=0, tiled=True)  237 us
    all_to_all x1, starting transfers between devices, shards(): lax.all_to_all(value_grad, 'head', split_axis=0, concat_axis=1, tiled=True)  116 us
    dot_general x96, matrix products, score_block(): jnp.einsum('qhd,khd->hqk', query_heads, key_block, preferred_element_type...  104 us
    dot_general x64, matrix products, block_terms(): jnp.einsum('hqk,khd->qhd', score_grad, key_block, preferred_element_type=...  67.8 us
    dot_general x64, matrix products, block_terms(): jnp.einsum('qhd,khd->hqk', upstream_heads, value_block, preferred_element...  66.3 us
    dot_general x32, matrix products, output_turn(): jnp.einsum('hqk,khd->qhd', weights_low, value_block, preferred_element_ty...  46 us
  transfers between devices with their start and end apart: 137, of which 136 were waited for; matrix products, arithmetic and copies ran while one was open for 11% of the time, Pallas kernels for 0%

commit v1 on v0

v1 whole, which is shorter than its diff:
```python
import functools
import math

import jax
import jax.numpy as jnp
from jax import lax
from jax.experimental import pallas as pl
from jax.experimental.pallas import tpu as pltpu
from jax.sharding import Mesh, PartitionSpec as P

DH = 128
HALF = 256
SCALING = 1.0 / math.sqrt(DH)
SCALING2 = SCALING * math.log2(math.e)
F32 = jnp.float32
BF16 = jnp.bfloat16
LINE = ("z",)
PLANE = ("yh", "x", "yl")
TOKENS = P(("x", "z", "yl", "yh", "c"), None)
VMEM_LIMIT = 56 << 20


def dot(a, b, ca, cb):
    return lax.dot_general(a, b, (((ca,), (cb,)), ((), ())), preferred_element_type=F32)


def head_columns(h):
    return slice(h * DH, (h + 1) * DH), slice(HALF + h * DH, HALF + (h + 1) * DH)


def forward_kernel(qg_ref, kv_ref, out_ref, stats_ref, vt_ref):
    @pl.when(pl.program_id(0) == 0)
    def _():
        vt_ref[...] = kv_ref[:, HALF:].T

    logs, deltas = [], []
    for h in range(2):
        a, b = head_columns(h)
        scores = dot(kv_ref[:, a], qg_ref[:, a], 1, 1)
        top = jnp.max(scores, axis=0, keepdims=True)
        weights = jnp.exp2((scores - top) * SCALING2)
        total = jnp.sum(weights, axis=0, keepdims=True)
        out_t = dot(vt_ref[a, :], weights.astype(BF16), 1, 0) * (1.0 / total)
        out_ref[:, a] = out_t.T.astype(BF16)
        logs.append(top * SCALING2 + jnp.log2(total))
        deltas.append(jnp.sum(qg_ref[:, b].T.astype(F32) * out_t, axis=0, keepdims=True))
    stats_ref[...] = jnp.concatenate(logs + deltas, 0)


def forward(qg, kv, block):
    nq, nk = qg.shape[0], kv.shape[0]
    return pl.pallas_call(
        forward_kernel,
        grid=(nq // block,),
        in_specs=[
            pl.BlockSpec((block, 2 * HALF), lambda i: (i, 0)),
            pl.BlockSpec((nk, 2 * HALF), lambda i: (0, 0)),
        ],
        out_specs=[
            pl.BlockSpec((block, HALF), lambda i: (i, 0)),
            pl.BlockSpec((4, block), lambda i: (0, i)),
        ],
        out_shape=[
            jax.ShapeDtypeStruct((nq, HALF), BF16),
            jax.ShapeDtypeStruct((4, nq), F32),
        ],
        scratch_shapes=[pltpu.VMEM((HALF, nk), BF16)],
        compiler_params=pltpu.CompilerParams(vmem_limit_bytes=VMEM_LIMIT),
        name="forward",
    )(qg, kv)


def backward_kernel(steps, qg_ref, kv_ref, stats_ref, dq_ref, dkv_ref, kt_ref, sum_ref):
    i = pl.program_id(0)

    @pl.when(i == 0)
    def _():
        kt_ref[...] = kv_ref[:, :HALF].T

    for h in range(2):
        a, b = head_columns(h)
        log_total = stats_ref[h : h + 1, :]
        delta = stats_ref[2 + h : 3 + h, :]
        scores = dot(kv_ref[:, a], qg_ref[:, a], 1, 1)
        weights = jnp.exp2(scores * SCALING2 - log_total)
        upstream_dot = dot(kv_ref[:, b], qg_ref[:, b], 1, 1)
        score_grad = (weights * (upstream_dot - delta)).astype(BF16)
        dv = dot(weights.astype(BF16), qg_ref[:, b], 1, 0)
        dk = dot(score_grad, qg_ref[:, a], 1, 0) * SCALING
        dq_ref[:, a] = (dot(kt_ref[a, :], score_grad, 1, 0) * SCALING).T.astype(BF16)

        @pl.when(i == 0)
        def _():
            sum_ref[:, a] = dk
            sum_ref[:, b] = dv

        @pl.when(i > 0)
        def _():
            sum_ref[:, a] += dk
            sum_ref[:, b] += dv

    @pl.when(i == steps - 1)
    def _():
        dkv_ref[...] = sum_ref[...].astype(BF16)


def backward(qg, kv, stats, block):
    nq, nk = qg.shape[0], kv.shape[0]
    return pl.pallas_call(
        functools.partial(backward_kernel, nq // block),
        grid=(nq // block,),
        in_specs=[
            pl.BlockSpec((block, 2 * HALF), lambda i: (i, 0)),
            pl.BlockSpec((nk, 2 * HALF), lambda i: (0, 0)),
            pl.BlockSpec((4, block), lambda i: (0, i)),
        ],
        out_specs=[
            pl.BlockSpec((block, HALF), lambda i: (i, 0)),
            pl.BlockSpec((nk, 2 * HALF), lambda i: (0, 0)),
        ],
        out_shape=[
            jax.ShapeDtypeStruct((nq, HALF), BF16),
            jax.ShapeDtypeStruct((nk, 2 * HALF), BF16),
        ],
        scratch_shapes=[pltpu.VMEM((HALF, nk), BF16), pltpu.VMEM((nk, 2 * HALF), F32)],
        compiler_params=pltpu.CompilerParams(vmem_limit_bytes=VMEM_LIMIT),
        name="backward",
    )(qg, kv, stats)


def to_other_core(x):
    return lax.ppermute(x, "c", [(0, 1), (1, 0)])


def everyone(x, axes):
    peers = lax.axis_size(axes)
    return lax.all_to_all(
        jnp.broadcast_to(x[None], (peers,) + x.shape), axes, split_axis=0, concat_axis=0, tiled=True
    )


def owners_sum(x, axes):
    peers = lax.axis_size(axes)
    terms = lax.all_to_all(
        x.reshape(peers, x.shape[0] // peers, x.shape[1]), axes, split_axis=0, concat_axis=0, tiled=True
    )
    return jnp.sum(terms.astype(F32), axis=0)


def shards(queries, keys, values, upstream):
    core = lax.axis_index("c")
    rows = queries.shape[0]

    def halves(x):
        mine = jnp.where(core == 0, x[:, :HALF], x[:, HALF:])
        theirs = jnp.where(core == 0, x[:, HALF:], x[:, :HALF])
        return mine, theirs

    parts = [halves(x) for x in (queries, upstream, keys, values)]
    mine = jnp.concatenate([p[0] for p in parts], 1)
    theirs = to_other_core(jnp.concatenate([p[1] for p in parts], 1))
    both = jnp.concatenate([mine, theirs], 0)
    qg = everyone(both[:, : 2 * HALF], LINE).reshape(-1, 2 * HALF)
    kv = everyone(both[:, 2 * HALF :], PLANE).reshape(-1, 2 * HALF)

    out_part, stats_part = forward(qg, kv, 512)
    stats_all = everyone(stats_part, LINE)
    logs = stats_all[:, :2]
    top = jnp.max(logs, axis=0)
    log_total = top + jnp.log2(jnp.sum(jnp.exp2(logs - top), axis=0))
    delta = jnp.sum(jnp.exp2(logs - log_total) * stats_all[:, 2:], axis=0)
    stats = jnp.concatenate([log_total, delta], 0)
    own_scale = jnp.exp2(stats_part[:2] - log_total).T
    out_scaled = (out_part.reshape(-1, 2, DH) * own_scale[:, :, None]).astype(BF16).reshape(-1, HALF)

    dq_part, dkv_part = backward(qg, kv, stats, 512)
    attended = owners_sum(out_scaled, LINE)
    dq = owners_sum(dq_part, LINE)
    dkv = owners_sum(dkv_part, PLANE)
    results = jnp.concatenate([attended, dq, dkv], 1).astype(BF16)
    own, away = results[:rows], to_other_core(results[rows:])

    def whole(n):
        a, b = own[:, n * HALF : (n + 1) * HALF], away[:, n * HALF : (n + 1) * HALF]
        return jnp.concatenate([jnp.where(core == 0, a, b), jnp.where(core == 0, b, a)], 1)

    return whole(0), whole(1), whole(2), whole(3)


def solution(mesh):
    fine = Mesh(mesh.devices.reshape(2, 2, 4, 8, 2), ("yh", "c", "x", "z", "yl"))
    return jax.shard_map(
        shards, mesh=fine, in_specs=(TOKENS,) * 4, out_specs=(TOKENS,) * 4, check_vma=False
    )
```

time: 1600 us -> 176 us (0.11)
  waiting for transfers between devices: 1080 us -> 24.6 us
  matrix products: 306 us -> 0 us
  starting transfers between devices: 152 us -> 17.2 us
  blocking collectives: 11 us -> 96.6 us
  Pallas kernels: 0 us -> 25.3 us
    ppermute x128 -> x2, waiting for transfers between devices: 560 us -> 1.97 us  [to_other_core(): return lax.ppermute(x, 'c', [(0, 1), (1, 0)])]
    all_gather x2 -> x0, waiting for transfers between devices: 498 us -> none  [the longest x1 260 us: shards(): piece_values = lax.all_gather(values_here, 'blk', axis=0, tiled=True)]
    dot_general x384 -> x0, matrix products: 306 us -> none  [the longest x96 104 us: score_block(): jnp.einsum('qhd,khd->hqk', query_heads, key_block, preferred_element_type...]
    all_to_all x7 -> x2, starting transfers between devices: 141 us -> 7.39 us  [owners_sum(): lax.all_to_all(x.reshape(peers, x.shape[0] // peers, x.shape[1]), axes, s...]
    all_to_all x1 -> x4, blocking collectives: 11 us -> 96.6 us  [the longest x3 77.8 us: everyone(): lax.all_to_all(jnp.broadcast_to(x[None], (peers,) + x.shape), axes, split...]
    pallas_call x0 -> x2, Pallas kernels: none -> 25.3 us  [the longest x1 15.9 us: backward(): pl.pallas_call(functools.partial(backward_kernel, nq // block), grid=(nq...]
  transfers between devices with their start and end apart: 137 -> 4, of which waited for: 136 -> 3; matrix products, arithmetic and copies ran while one was open for 11% -> 0% of each run, Pallas kernels for 0% -> 9%
where the time goes in v1:
time: 176 us; the launch traced here: 175 us
  blocking collectives  96.6 us (55%)
  Pallas kernels  25.3 us (14%)
  waiting for transfers between devices  24.6 us (14%)
  starting transfers between devices  17.2 us (10%)
  other arithmetic  7.18 us (4%)
  local copies, waits for them, and re-layouts  3.33 us (2%)
    all_to_all x3, blocking collectives, everyone(): lax.all_to_all(jnp.broadcast_to(x[None], (peers,) + x.shape), axes, split...  77.8 us
    all_to_all x2, waiting for transfers between devices, owners_sum(): lax.all_to_all(x.reshape(peers, x.shape[0] // peers, x.shape[1]), axes, s...  22.6 us
    all_to_all x1, blocking collectives, owners_sum(): lax.all_to_all(x.reshape(peers, x.shape[0] // peers, x.shape[1]), axes, s...  18.8 us
    pallas_call x1, Pallas kernels, backward(): pl.pallas_call(functools.partial(backward_kernel, nq // block), grid=(nq...  15.9 us
    ppermute x2, starting transfers between devices, to_other_core(): return lax.ppermute(x, 'c', [(0, 1), (1, 0)])  9.85 us
    pallas_call x1, Pallas kernels, forward(): pl.pallas_call(forward_kernel, grid=(nq // block,), in_specs=[pl.BlockSpe...  9.36 us
    all_to_all x2, starting transfers between devices, owners_sum(): lax.all_to_all(x.reshape(peers, x.shape[0] // peers, x.shape[1]), axes, s...  7.39 us
  transfers between devices with their start and end apart: 4, of which 3 were waited for; matrix products, arithmetic and copies ran while one was open for 0% of the time, Pallas kernels for 9%

profile of v1, /device:TPU:1, one launch (start us, length us, event | category | flops | bytes accessed | tf_op | source)
XLA Modules:
  0.0 175.0 jit_solution(1317103004217799572)
XLA Ops:
  0.6 0.8 broadcast_select_fusion.14
  1.5 0.8 broadcast_select_fusion.12
  2.3 3.3 %collective-permute-start = (bf16[64,1024]{1,0:T(8,128)(2,1)S(1)}, bf16[64,1024]{1,0:T(8,128)(2,1)S(1)}, u32[]{:S(2)}, u32[]{:S(2)}) collective-permute-start(bf16[64,1024]{1,0:T(8,128)(2,1)S(1)} %pad_maximum_fusion.3), channel_id=1, source_target_pairs={{0,64},{64,0},{1,65},{65,1},{2,66},{66,2},{3,67},{67,3},{4,68},{68... | collective-permute-start | bytes 393224 | tf_op jit(solution)/shard_map/ppermute | solution.py:132
  5.6 1.0 collective-permute-done
  6.7 0.1 broadcast_in_dim.6
  6.8 34.3 %all_to_all.30 = bf16[8,128,512]{2,1,0:T(8,128)(2,1)} all-to-all(bf16[8,128,512]{2,1,0:T(8,128)(2,1)S(1)} %broadcast_in_dim.6), channel_id=1, replica_groups=mesh['yh'=2,'c'=2,'x'=4,'z'=8,'yl'=2] {'z'}, dimensions={0} | all-to-all | bytes 2097152 | tf_op jit(solution)/shard_map/all_to_all | solution.py:137
  41.1 0.2 broadcast_in_dim.7
  41.3 33.1 %all_to_all.31 = bf16[16,128,512]{2,1,0:T(8,128)(2,1)} all-to-all(bf16[16,128,512]{2,1,0:T(8,128)(2,1)S(1)} %broadcast_in_dim.7), channel_id=1, replica_groups=mesh['yh'=2,'c'=2,'x'=4,'z'=8,'yl'=2] {'yh','x','yl'}, dimensions={0} | all-to-all | bytes 4194304 | tf_op jit(solution)/shard_map/all_to_all | solution.py:137
  74.5 9.4 %forward.1 = (bf16[1024,256]{1,0:T(8,128)(2,1)}, f32[4,1024]{1,0:T(4,128)}) custom-call(bf16[1024,512]{1,0:T(8,128)(2,1)} %bitcast.10, bf16[2048,512]{1,0:T(8,128)(2,1)} %bitcast.8), custom_call_target="tpu_custom_call" | custom-call | tf_op jit(solution)/shard_map/forward/pallas_call | solution.py:52
  83.8 0.7 broadcast_in_dim.8
  84.6 10.3 %all_to_all.32 = f32[8,4,1024]{2,1,0:T(4,128)S(1)} all-to-all(f32[8,4,1024]{2,1,0:T(4,128)S(1)} %broadcast_in_dim.8), channel_id=1, replica_groups=mesh['yh'=2,'c'=2,'x'=4,'z'=8,'yl'=2] {'z'}, dimensions={0} | all-to-all | bytes 262144 | tf_op jit(solution)/shard_map/all_to_all | solution.py:137
  94.9 0.1 slice_reduce_fusion
  94.9 0.1 exponential_reduce_fusion
  95.0 0.7 exponential_bitcast_fusion
  95.7 0.0 copy-start
  95.7 0.2 copy.15
  96.0 1.2 mul.14
  97.2 0.8 mul.15
  98.1 0.0 copy-done
  98.1 0.9 fusion
  99.0 3.7 %all-to-all-start.3 = ((bf16[8,128,256]{2,1,0:T(8,128)(2,1)}), bf16[8,128,256]{2,1,0:T(8,128)(2,1)S(1)}, u32[]{:S(2)}, u32[]{:S(2)}) async-start(bf16[8,128,256]{2,1,0:T(8,128)(2,1)} %fusion), calls=%async_computation.3 | async-start | bytes 1048576 | tf_op jit(solution)/shard_map/all_to_all | solution.py:144
  102.7 0.1 fusion.1
  102.8 0.6 pad_maximum_fusion.8.stats_ref
  103.4 15.9 %backward.1 = (bf16[1024,256]{1,0:T(8,128)(2,1)}, bf16[2048,512]{1,0:T(8,128)(2,1)}) custom-call(bf16[1024,512]{1,0:T(8,128)(2,1)} %bitcast.11, bf16[2048,512]{1,0:T(8,128)(2,1)} %bitcast.9, f32[4,1024]{1,0:T(4,128)} %pad_maximum_fusion.8.stats_ref), custom_call_target="tpu_custom_call" | custom-call | tf_op jit(solution)/shard_map/backward/pallas_call | solution.py:109
  119.3 0.0 all-to-all-done.3
  119.3 18.8 %all_to_all.33 = bf16[8,128,256]{2,1,0:T(8,128)(2,1)S(1)} all-to-all(bf16[8,128,256]{2,1,0:T(8,128)(2,1)} %bitcast.13), channel_id=1, replica_groups=mesh['yh'=2,'c'=2,'x'=4,'z'=8,'yl'=2] {'z'}, dimensions={0} | all-to-all | bytes 1048576 | tf_op jit(solution)/shard_map/all_to_all | solution.py:144
  138.1 3.7 %all-to-all-start.5 = ((bf16[16,128,512]{2,1,0:T(8,128)(2,1)}), bf16[16,128,512]{2,1,0:T(8,128)(2,1)S(1)}, u32[]{:S(2)}, u32[]{:S(2)}) async-start(bf16[16,128,512]{2,1,0:T(8,128)(2,1)} %bitcast.12), calls=%async_computation.5 | async-start | bytes 4194304 | tf_op jit(solution)/shard_map/all_to_all | solution.py:144
  141.9 0.1 reduce
  141.9 0.1 reduce.1
  142.0 22.6 %all-to-all-done.5 = bf16[16,128,512]{2,1,0:T(8,128)(2,1)S(1)} async-done(((bf16[16,128,512]{2,1,0:T(8,128)(2,1)}), bf16[16,128,512]{2,1,0:T(8,128)(2,1)S(1)}, u32[]{:S(2)}, u32[]{:S(2)}) %all-to-all-start.5) | async-done | bytes 2097184 | tf_op jit(solution)/shard_map/all_to_all | solution.py:144
  164.6 0.3 reduce.2
  164.9 6.5 %collective-permute-start.1 = (bf16[64,1024]{1,0:T(8,128)(2,1)S(1)}, bf16[64,1024]{1,0:T(8,128)(2,1)S(1)}, u32[]{:S(2)}, u32[]{:S(2)}) collective-permute-start(bf16[64,1024]{1,0:T(8,128)(2,1)S(1)} %pad_maximum_fusion.1), channel_id=1, source_target_pairs={{0,64},{64,0},{1,65},{65,1},{2,66},{66,2},{3,67},{67,3},{4,68},{68... | collective-permute-start | bytes 393224 | tf_op jit(solution)/shard_map/ppermute | solution.py:132
  171.5 1.0 collective-permute-done.1
  172.5 0.6 pad_maximum_fusion.7
  173.1 0.6 pad_maximum_fusion.6
  173.7 0.6 pad_maximum_fusion.5
  174.4 0.6 pad_maximum_fusion.4
  (5 shorter events, 0.1 us)
Async XLA Ops:
  2.3 4.3 %collective-permute-start = (bf16[64,1024]{1,0:T(8,128)(2,1)S(1)}, bf16[64,1024]{1,0:T(8,128)(2,1)S(1)}, u32[]{:S(2)}, u32[]{:S(2)}) collective-permute-start(bf16[64,1024]{1,0:T(8,128)(2,1)S(1)} %pad_maximum_fusion.3), channel_id=1, source_target_pairs={{0,64},{64,0},{1,65},{65,1},{2,66},{66,2},{3,67},{67,3},{4,68},{68... | collective-permute-start | bytes 393224 | tf_op jit(solution)/shard_map/ppermute | solution.py:132
  95.7 2.3 %copy-start = (bf16[1024,256]{1,0:T(8,128)(2,1)S(1)}, bf16[1024,256]{1,0:T(8,128)(2,1)}, u32[]{:S(2)}) copy-start(bf16[1024,256]{1,0:T(8,128)(2,1)} %get-tuple-element.8) | copy-start | bytes 1572868
  99.0 20.3 %all-to-all-start.3 = ((bf16[8,128,256]{2,1,0:T(8,128)(2,1)}), bf16[8,128,256]{2,1,0:T(8,128)(2,1)S(1)}, u32[]{:S(2)}, u32[]{:S(2)}) async-start(bf16[8,128,256]{2,1,0:T(8,128)(2,1)} %fusion), calls=%async_computation.3 | async-start | bytes 1048576 | tf_op jit(solution)/shard_map/all_to_all | solution.py:144
  138.1 26.5 %all-to-all-start.5 = ((bf16[16,128,512]{2,1,0:T(8,128)(2,1)}), bf16[16,128,512]{2,1,0:T(8,128)(2,1)S(1)}, u32[]{:S(2)}, u32[]{:S(2)}) async-start(bf16[16,128,512]{2,1,0:T(8,128)(2,1)} %bitcast.12), calls=%async_computation.5 | async-start | bytes 4194304 | tf_op jit(solution)/shard_map/all_to_all | solution.py:144
  164.9 7.5 %collective-permute-start.1 = (bf16[64,1024]{1,0:T(8,128)(2,1)S(1)}, bf16[64,1024]{1,0:T(8,128)(2,1)S(1)}, u32[]{:S(2)}, u32[]{:S(2)}) collective-permute-start(bf16[64,1024]{1,0:T(8,128)(2,1)S(1)} %pad_maximum_fusion.1), channel_id=1, source_target_pairs={{0,64},{64,0},{1,65},{65,1},{2,66},{66,2},{3,67},{67,3},{4,68},{68... | collective-permute-start | bytes 393224 | tf_op jit(solution)/shard_map/ppermute | solution.py:132

commit v2 on v1

v2 whole, which is shorter than its diff:
```python
import functools
import math

import jax
import jax.numpy as jnp
from jax import lax
from jax.experimental import pallas as pl
from jax.experimental.pallas import tpu as pltpu
from jax.sharding import Mesh, PartitionSpec as P

DH = 128
HALF = 256
SCALING = 1.0 / math.sqrt(DH)
SCALING2 = SCALING * math.log2(math.e)
F32 = jnp.float32
BF16 = jnp.bfloat16
LINE = "z"
PLANE = ("yh", "x", "yl")
TOKENS = P(("x", "z", "yl", "yh", "c"), None)
VMEM_LIMIT = 56 << 20
BLOCK = 512
IN_VMEM = pl.BlockSpec(memory_space=pltpu.VMEM)
IN_SMEM = pl.BlockSpec(memory_space=pltpu.SMEM)


def dot(a, b, ca, cb):
    return lax.dot_general(a, b, (((ca,), (cb,)), ((), ())), preferred_element_type=F32)


def head_columns(h):
    return slice(h * DH, (h + 1) * DH), slice(HALF + h * DH, HALF + (h + 1) * DH)


def line_rows(z, step, size, rows):
    return pl.ds(pl.multiple_of(lax.rem(z + (step + size), size) * rows, rows), rows)


def forward_kernel(steps, z_ref, *refs):
    pieces, (kv_ref, out_ref, stats_ref, qg_ref, vt_ref) = refs[: len(steps)], refs[len(steps) :]
    rows = pieces[0].shape[0]
    for step, piece in zip(steps, pieces):
        qg_ref[line_rows(z_ref[0], step, len(steps), rows), :] = piece[...]
    vt_ref[...] = kv_ref[:, HALF:].T

    def block(i, carry):
        here = pl.ds(pl.multiple_of(i * BLOCK, BLOCK), BLOCK)
        logs, deltas = [], []
        for h in range(2):
            a, b = head_columns(h)
            scores = dot(kv_ref[:, a], qg_ref[here, a], 1, 1)
            top = jnp.max(scores, axis=0, keepdims=True)
            weights = jnp.exp2((scores - top) * SCALING2)
            total = jnp.sum(weights, axis=0, keepdims=True)
            out_t = dot(vt_ref[a, :], weights.astype(BF16), 1, 0) * (1.0 / total)
            out_ref[here, a] = out_t.T.astype(BF16)
            logs.append(top * SCALING2 + jnp.log2(total))
            deltas.append(jnp.sum(qg_ref[here, b].T.astype(F32) * out_t, axis=0, keepdims=True))
        stats = jnp.concatenate(logs + deltas, 0)
        for peer in range(stats_ref.shape[0]):
            stats_ref[peer, :, here] = stats
        return carry

    lax.fori_loop(0, qg_ref.shape[0] // BLOCK, block, 0)


def forward(z, steps, pieces, kv):
    nq, nk = pieces[0].shape[0] * len(steps), kv.shape[0]
    return pl.pallas_call(
        functools.partial(forward_kernel, steps),
        in_specs=[IN_SMEM] + [IN_VMEM] * (len(steps) + 1),
        out_specs=[IN_VMEM] * 3,
        out_shape=[
            jax.ShapeDtypeStruct((nq, HALF), BF16),
            jax.ShapeDtypeStruct((len(steps), 4, nq), F32),
            jax.ShapeDtypeStruct((nq, 2 * HALF), BF16),
        ],
        scratch_shapes=[pltpu.VMEM((HALF, nk), BF16)],
        compiler_params=pltpu.CompilerParams(vmem_limit_bytes=VMEM_LIMIT),
        name="forward",
    )(z, *pieces, kv)


def backward_kernel(steps, z_ref, qg_ref, kv_ref, stats_ref, *refs):
    dq_refs, (dkv_ref, dq_ref, kt_ref, sum_ref, merged_ref) = refs[: len(steps)], refs[len(steps) :]
    kt_ref[...] = kv_ref[:, :HALF].T
    logs = [stats_ref[j, 0:2, :] for j in range(len(steps))]
    top = functools.reduce(jnp.maximum, logs)
    log_total = top + jnp.log2(sum(jnp.exp2(x - top) for x in logs))
    merged_ref[0:2, :] = log_total
    merged_ref[2:4, :] = sum(
        jnp.exp2(x - log_total) * stats_ref[j, 2:4, :] for j, x in enumerate(logs)
    )
    sum_ref[...] = jnp.zeros_like(sum_ref)

    def block(i, carry):
        here = pl.ds(pl.multiple_of(i * BLOCK, BLOCK), BLOCK)
        for h in range(2):
            a, b = head_columns(h)
            log_total = merged_ref[h : h + 1, here]
            delta = merged_ref[2 + h : 3 + h, here]
            scores = dot(kv_ref[:, a], qg_ref[here, a], 1, 1)
            weights = jnp.exp2(scores * SCALING2 - log_total)
            upstream_dot = dot(kv_ref[:, b], qg_ref[here, b], 1, 1)
            score_grad = (weights * (upstream_dot - delta)).astype(BF16)
            sum_ref[:, b] += dot(weights.astype(BF16), qg_ref[here, b], 1, 0)
            sum_ref[:, a] += dot(score_grad, qg_ref[here, a], 1, 0) * SCALING
            dq_ref[here, a] = (dot(kt_ref[a, :], score_grad, 1, 0) * SCALING).T
        return carry

    lax.fori_loop(0, qg_ref.shape[0] // BLOCK, block, 0)
    dkv_ref[...] = sum_ref[...].astype(BF16)
    for step, ref in zip(steps, dq_refs):
        ref[...] = dq_ref[line_rows(z_ref[0], step, len(steps), ref.shape[0]), :]


def backward(z, steps, qg, kv, stats):
    nq, nk = qg.shape[0], kv.shape[0]
    out = pl.pallas_call(
        functools.partial(backward_kernel, steps),
        in_specs=[IN_SMEM] + [IN_VMEM] * 3,
        out_specs=[IN_VMEM] * (len(steps) + 1),
        out_shape=[jax.ShapeDtypeStruct((nq // len(steps), HALF), F32)] * len(steps)
        + [jax.ShapeDtypeStruct((nk, 2 * HALF), BF16)],
        scratch_shapes=[
            pltpu.VMEM((nq, HALF), F32),
            pltpu.VMEM((HALF, nk), BF16),
            pltpu.VMEM((nk, 2 * HALF), F32),
            pltpu.VMEM((4, nq), F32),
        ],
        compiler_params=pltpu.CompilerParams(vmem_limit_bytes=VMEM_LIMIT),
        name="backward",
    )(z, qg, kv, stats)
    return dict(zip(steps, out[:-1])), out[-1]


def to_other_core(x):
    return lax.ppermute(x, "c", [(0, 1), (1, 0)])


def along_line(x, by):
    size = lax.axis_size(LINE)
    return lax.ppermute(x, LINE, [(i, (i + by) % size) for i in range(size)])


def exchange(x, axes):
    return lax.all_to_all(x, axes, split_axis=0, concat_axis=0, tiled=True)


def shards(queries, keys, values, upstream):
    core = lax.axis_index("c")
    z = lax.axis_index(LINE).astype(jnp.int32).reshape(1)
    line = lax.axis_size(LINE)
    plane = lax.axis_size(PLANE)
    rows = queries.shape[0]

    def both_cores(*arrays):
        mine = [jnp.where(core == 0, x[:, :HALF], x[:, HALF:]) for x in arrays]
        theirs = [jnp.where(core == 0, x[:, HALF:], x[:, :HALF]) for x in arrays]
        away = to_other_core(jnp.concatenate(theirs, 1))
        return jnp.concatenate([jnp.concatenate(mine, 1), away], 0)

    kv = both_cores(keys, values)
    kv = exchange(jnp.broadcast_to(kv[None], (plane,) + kv.shape), PLANE).reshape(-1, 2 * HALF)
    pieces = {0: both_cores(queries, upstream)}
    for step in range(1, line // 2 + 1):
        pieces[-step] = along_line(pieces[1 - step], 1)
        if step < line // 2:
            pieces[step] = along_line(pieces[step - 1], -1)
    steps = sorted(pieces)

    out_part, stats_part, qg = forward(z, steps, [pieces[s] for s in steps], kv)
    stats = exchange(stats_part, LINE)
    out_parts = exchange(out_part.reshape(line, -1, HALF), LINE)

    dq_parts, dkv_part = backward(z, steps, qg, kv, stats)
    dkv_parts = exchange(dkv_part.reshape(plane, -1, 2 * HALF), PLANE)
    dq_up, dq_down = dq_parts[-line // 2], dq_parts[line // 2 - 1]
    dq_up = along_line(dq_up, -1)
    for step in range(line // 2 - 1, 0, -1):
        dq_up = along_line(dq_up + dq_parts[-step], -1)
        dq_down = along_line(dq_down, 1)
        if step > 1:
            dq_down = dq_down + dq_parts[step - 1]
    dq = dq_parts[0] + dq_up + dq_down

    own = lax.dynamic_slice_in_dim(stats[:, 0:2, :], z[0] * 2 * rows, 2 * rows, 2)
    top = jnp.max(own, axis=0)
    share = jnp.exp2(own - (top + jnp.log2(jnp.sum(jnp.exp2(own - top), axis=0))))
    share = jnp.repeat(share.transpose(0, 2, 1), DH, axis=2)
    attended = jnp.sum(out_parts.astype(F32) * share, axis=0)
    dkv = jnp.sum(dkv_parts.astype(F32), axis=0)
    results = jnp.concatenate([attended, dq, dkv], 1).astype(BF16)
    kept, away = results[:rows], to_other_core(results[rows:])

    def whole(n):
        a, b = kept[:, n * HALF : (n + 1) * HALF], away[:, n * HALF : (n + 1) * HALF]
        return jnp.concatenate([jnp.where(core == 0, a, b), jnp.where(core == 0, b, a)], 1)

    return whole(0), whole(1), whole(2), whole(3)


def solution(mesh):
    fine = Mesh(mesh.devices.reshape(2, 2, 4, 8, 2), ("yh", "c", "x", "z", "yl"))
    return jax.shard_map(
        shards, mesh=fine, in_specs=(TOKENS,) * 4, out_specs=(TOKENS,) * 4, check_vma=False
    )
```

time: 176 us -> 132 us (0.75)
  blocking collectives: 96.6 us -> 16.2 us
  starting transfers between devices: 17.2 us -> 47.4 us
  local copies, waits for them, and re-layouts: 3.33 us -> 7.98 us
    all_to_all x4 -> x1, blocking collectives: 96.6 us -> 16.2 us  [exchange(): return lax.all_to_all(x, axes, split_axis=0, concat_axis=0, tiled=True)]
    ppermute x0 -> x14, starting transfers between devices: none -> 23.7 us  [along_line(): return lax.ppermute(x, LINE, [(i, (i + by) % size) for i in range(size)])]
    ppermute x0 -> x14, waiting for transfers between devices: none -> 19.7 us  [along_line(): return lax.ppermute(x, LINE, [(i, (i + by) % size) for i in range(size)])]
    all_to_all x2 -> x3, waiting for transfers between devices: 22.6 us -> 3.78 us  [exchange(): return lax.all_to_all(x, axes, split_axis=0, concat_axis=0, tiled=True)]
    all_to_all x2 -> x3, starting transfers between devices: 7.39 us -> 12.5 us  [exchange(): return lax.all_to_all(x, axes, split_axis=0, concat_axis=0, tiled=True)]
    broadcast_in_dim x3 -> x2, local copies, waits for them, and re-layouts: 1.01 us -> 3.6 us  [the longest x1 2.04 us: shards(): share = jnp.repeat(share.transpose(0, 2, 1), DH, axis=2)]
    mul x2 -> x0, local copies, waits for them, and re-layouts: 2.07 us -> none  [shards(): out_part.reshape(-1, 2, DH) * own_scale[:, :, None]]
    unnamed x2 -> x42, local copies, waits for them, and re-layouts: 0.01 us -> 2.08 us
  transfers between devices with their start and end apart: 4 -> 20, of which waited for: 3 -> 12; matrix products, arithmetic and copies ran while one was open for 0% -> 6% of each run, Pallas kernels for 9% -> 11%
where the time goes in v2:
time: 132 us; the launch traced here: 131 us
  starting transfers between devices  47.4 us (36%)
  waiting for transfers between devices  26.2 us (20%)
  Pallas kernels  24.8 us (19%)
  blocking collectives  16.2 us (12%)
  local copies, waits for them, and re-layouts  7.98 us (6%)
  other arithmetic  7.27 us (6%)
    ppermute x14, starting transfers between devices, along_line(): return lax.ppermute(x, LINE, [(i, (i + by) % size) for i in range(size)])  23.7 us
    ppermute x14, waiting for transfers between devices, along_line(): return lax.ppermute(x, LINE, [(i, (i + by) % size) for i in range(size)])  19.7 us
    all_to_all x1, blocking collectives, exchange(): return lax.all_to_all(x, axes, split_axis=0, concat_axis=0, tiled=True)  16.2 us
    pallas_call x1, Pallas kernels, backward(): pl.pallas_call(functools.partial(backward_kernel, steps), in_specs=[IN_SM...  14.6 us
    all_to_all x3, starting transfers between devices, exchange(): return lax.all_to_all(x, axes, split_axis=0, concat_axis=0, tiled=True)  12.5 us
    ppermute x3, starting transfers between devices, to_other_core(): return lax.ppermute(x, 'c', [(0, 1), (1, 0)])  11.1 us
    pallas_call x1, Pallas kernels, forward(): pl.pallas_call(functools.partial(forward_kernel, steps), in_specs=[IN_SME...  10.2 us
    all_to_all x3, waiting for transfers between devices, exchange(): return lax.all_to_all(x, axes, split_axis=0, concat_axis=0, tiled=True)  3.78 us
  transfers between devices with their start and end apart: 20, of which 12 were waited for; matrix products, arithmetic and copies ran while one was open for 6% of the time, Pallas kernels for 11%

profile of v2, /device:TPU:1, one launch (start us, length us, event | category | flops | bytes accessed | tf_op | source)
XLA Modules:
  0.0 130.9 jit_solution(11122584870604884660)
XLA Ops:
  0.6 0.8 broadcast_select_fusion.10
  1.5 3.3 %collective-permute-start.8 = (bf16[64,512]{1,0:T(8,128)(2,1)S(1)}, bf16[64,512]{1,0:T(8,128)(2,1)S(1)}, u32[]{:S(2)}, u32[]{:S(2)}) collective-permute-start(bf16[64,512]{1,0:T(8,128)(2,1)S(1)} %pad_maximum_fusion.5), channel_id=1, source_target_pairs={{0,64},{64,0},{1,65},{65,1},{2,66},{66,2},{3,67},{67,3},{4,68},{68... | collective-permute-start | bytes 196616 | tf_op jit(solution)/shard_map/ppermute | solution.py:137
  4.8 0.9 collective-permute-done.8
  5.7 1.6 %broadcast_in_dim.4 = bf16[16,128,512]{2,1,0:T(8,128)(2,1)} broadcast(bf16[128,512]{1,0:T(8,128)(2,1)S(1)} %pad_maximum_fusion.3), dimensions={1,2} | broadcast | bytes 2228224 | tf_op jit(solution)/shard_map/broadcast_in_dim | solution.py:163
  7.3 5.2 %all-to-all-start = ((bf16[16,128,512]{2,1,0:T(8,128)(2,1)}), bf16[16,128,512]{2,1,0:T(8,128)(2,1)S(1)}, u32[]{:S(2)}, u32[]{:S(2)}) async-start(bf16[16,128,512]{2,1,0:T(8,128)(2,1)} %broadcast_in_dim.4), calls=%async_computation | async-start | bytes 4194304 | tf_op jit(solution)/shard_map/all_to_all | solution.py:146
  12.5 0.7 collective-permute-start
  13.2 0.9 collective-permute-done
  14.1 1.7 %collective-permute-start.1 = (bf16[128,512]{1,0:T(8,128)(2,1)S(1)}, bf16[128,512]{1,0:T(8,128)(2,1)S(1)}, u32[]{:S(2)}, u32[]{:S(2)}) collective-permute-start(bf16[128,512]{1,0:T(8,128)(2,1)S(1)} %pad_maximum_fusion.2.refs_4_), channel_id=1, source_target_pairs={{0,2},{2,4},{4,6},{6,8},{8,10},{10,12},{12,14},{14,0},{1,3},{3,5},... | collective-permute-start | bytes 393224 | tf_op jit(solution)/shard_map/ppermute | solution.py:142
  15.9 4.0 %collective-permute-start.5 = (bf16[128,512]{1,0:T(8,128)(2,1)S(1)}, bf16[128,512]{1,0:T(8,128)(2,1)S(1)}, u32[]{:S(2)}, u32[]{:S(2)}) collective-permute-start(bf16[128,512]{1,0:T(8,128)(2,1)S(1)} %pad_maximum_fusion.2.refs_4_), channel_id=1, source_target_pairs={{0,14},{2,0},{4,2},{6,4},{8,6},{10,8},{12,10},{14,12},{1,15},{3,1}... | collective-permute-start | bytes 393224 | tf_op jit(solution)/shard_map/ppermute | solution.py:142
  19.9 3.5 %collective-permute-done.1.refs_3_ = bf16[128,512]{1,0:T(8,128)(2,1)S(1)} collective-permute-done((bf16[128,512]{1,0:T(8,128)(2,1)S(1)}, bf16[128,512]{1,0:T(8,128)(2,1)S(1)}, u32[]{:S(2)}, u32[]{:S(2)}) %collective-permute-start.1) | collective-permute-done | bytes 131104 | tf_op jit(solution)/shard_map/ppermute | solution.py:142
  23.4 0.0 collective-permute-start.2
  23.4 0.0 collective-permute-done.5.refs_5_
  23.4 0.0 copy-start.11
  23.4 2.7 %collective-permute-start.6 = (bf16[128,512]{1,0:T(8,128)(2,1)S(1)}, bf16[128,512]{1,0:T(8,128)(2,1)S(1)}, u32[]{:S(2)}, u32[]{:S(2)}) collective-permute-start(bf16[128,512]{1,0:T(8,128)(2,1)S(1)} %collective-permute-done.5.refs_5_), channel_id=1, source_target_pairs={{0,14},{2,0},{4,2},{6,4},{8,6},{10,8},{12,10},{14,12},{1,15},{3,1}... | collective-permute-start | bytes 393224 | tf_op jit(solution)/shard_map/ppermute | solution.py:142
  26.1 2.7 %collective-permute-done.2.refs_2_ = bf16[128,512]{1,0:T(8,128)(2,1)S(1)} collective-permute-done((bf16[128,512]{1,0:T(8,128)(2,1)S(1)}, bf16[128,512]{1,0:T(8,128)(2,1)S(1)}, u32[]{:S(2)}, u32[]{:S(2)}) %collective-permute-start.2) | collective-permute-done | bytes 131104 | tf_op jit(solution)/shard_map/ppermute | solution.py:142
  28.7 0.0 collective-permute-start.3
  28.8 0.0 collective-permute-done.6.refs_6_
  28.8 2.7 %collective-permute-start.7 = (bf16[128,512]{1,0:T(8,128)(2,1)S(1)}, bf16[128,512]{1,0:T(8,128)(2,1)S(1)}, u32[]{:S(2)}, u32[]{:S(2)}) collective-permute-start(bf16[128,512]{1,0:T(8,128)(2,1)S(1)} %collective-permute-done.6.refs_6_), channel_id=1, source_target_pairs={{0,14},{2,0},{4,2},{6,4},{8,6},{10,8},{12,10},{14,12},{1,15},{3,1}... | collective-permute-start | bytes 393224 | tf_op jit(solution)/shard_map/ppermute | solution.py:142
  31.4 2.6 %collective-permute-done.3.refs_1_ = bf16[128,512]{1,0:T(8,128)(2,1)S(1)} collective-permute-done((bf16[128,512]{1,0:T(8,128)(2,1)S(1)}, bf16[128,512]{1,0:T(8,128)(2,1)S(1)}, u32[]{:S(2)}, u32[]{:S(2)}) %collective-permute-start.3) | collective-permute-done | bytes 131104 | tf_op jit(solution)/shard_map/ppermute | solution.py:142
  34.1 0.0 collective-permute-start.4
  34.1 0.0 collective-permute-done.7.refs_7_
  34.1 5.3 %collective-permute-done.4.refs_0_ = bf16[128,512]{1,0:T(8,128)(2,1)S(1)} collective-permute-done((bf16[128,512]{1,0:T(8,128)(2,1)S(1)}, bf16[128,512]{1,0:T(8,128)(2,1)S(1)}, u32[]{:S(2)}, u32[]{:S(2)}) %collective-permute-start.4) | collective-permute-done | bytes 131104 | tf_op jit(solution)/shard_map/ppermute | solution.py:142
  39.4 3.8 %all-to-all-done = bf16[16,128,512]{2,1,0:T(8,128)(2,1)S(1)} async-done(((bf16[16,128,512]{2,1,0:T(8,128)(2,1)}), bf16[16,128,512]{2,1,0:T(8,128)(2,1)S(1)}, u32[]{:S(2)}, u32[]{:S(2)}) %all-to-all-start) | async-done | bytes 2097184 | tf_op jit(solution)/shard_map/all_to_all | solution.py:146
  43.2 0.0 copy-done.10
  43.2 0.0 copy-done.12
  43.2 0.0 copy-done.13
  43.2 0.0 copy-done.14
  43.2 1.3 copy-done
  44.5 10.2 %forward.1 = (bf16[1024,256]{1,0:T(8,128)(2,1)}, f32[8,4,1024]{2,1,0:T(4,128)}, bf16[1024,512]{1,0:T(8,128)(2,1)}) custom-call(s32[1]{0:T(128)} %bitcast.z_ref, bf16[128,512]{1,0:T(8,128)(2,1)} %copy-done.16, bf16[128,512]{1,0:T(8,128)(2,1)} %copy-done.14, bf16[128,512]{1,0:T(8,128)(2,1)} %copy-done.12, bf16[128,512]{1,0:T(8,128)(2,1)} %copy-done.10, ...), custom_call_target="tpu_custom_call" | custom-call | tf_op jit(solution)/shard_map/forward/pallas_call | solution.py:68
  54.7 16.2 %all_to_all.20.stats_ref = f32[8,4,1024]{2,1,0:T(4,128)} all-to-all(f32[8,4,1024]{2,1,0:T(4,128)} %get-tuple-element.17), channel_id=1, replica_groups=mesh['yh'=2,'c'=2,'x'=4,'z'=8,'yl'=2] {'z'}, dimensions={0} | all-to-all | bytes 262144 | tf_op jit(solution)/shard_map/all_to_all | solution.py:146
  71.0 3.7 %all-to-all-start.1 = ((bf16[8,128,256]{2,1,0:T(8,128)(2,1)}), bf16[8,128,256]{2,1,0:T(8,128)(2,1)S(1)}, u32[]{:S(2)}, u32[]{:S(2)}) async-start(bf16[8,128,256]{2,1,0:T(8,128)(2,1)} %bitcast.9), calls=%async_computation.1 | async-start | bytes 1048576 | tf_op jit(solution)/shard_map/all_to_all | solution.py:146
  74.7 14.6 %backward.1 = (f32[128,256]{1,0:T(8,128)}, f32[128,256]{1,0:T(8,128)}, f32[128,256]{1,0:T(8,128)}, f32[128,256]{1,0:T(8,128)}, f32[128,256]{1,0:T(8,128)}, /*ind...) custom-call(s32[1]{0:T(128)} %bitcast.z_ref, ...), custom_call_target="tpu_custom_call" | custom-call | tf_op jit(solution)/shard_map/backward/pallas_call | solution.py:118
  89.3 0.0 all-to-all-done.1
  89.4 0.7 copy-done.1
  90.1 3.7 %all-to-all-start.3 = ((bf16[16,128,512]{2,1,0:T(8,128)(2,1)}), bf16[16,128,512]{2,1,0:T(8,128)(2,1)S(1)}, u32[]{:S(2)}, u32[]{:S(2)}) async-start(bf16[16,128,512]{2,1,0:T(8,128)(2,1)} %bitcast.8), calls=%async_computation.3 | async-start | bytes 4194304 | tf_op jit(solution)/shard_map/all_to_all | solution.py:146
  93.8 2.5 %collective-permute-start.9 = (f32[128,256]{1,0:T(8,128)S(1)}, f32[128,256]{1,0:T(8,128)S(1)}, u32[]{:S(2)}, u32[]{:S(2)}) collective-permute-start(f32[128,256]{1,0:T(8,128)S(1)} %copy-done.20), channel_id=1, source_target_pairs={{0,14},{2,0},{4,2},{6,4},{8,6},{10,8},{12,10},{14,12},{1,15},{3,1}... | collective-permute-start | bytes 393224 | tf_op jit(solution)/shard_map/ppermute | solution.py:142
  96.3 0.0 collective-permute-start.13
  96.3 1.9 %collective-permute-done.9 = f32[128,256]{1,0:T(8,128)S(1)} collective-permute-done((f32[128,256]{1,0:T(8,128)S(1)}, f32[128,256]{1,0:T(8,128)S(1)}, u32[]{:S(2)}, u32[]{:S(2)}) %collective-permute-start.9) | collective-permute-done | bytes 131104 | tf_op jit(solution)/shard_map/ppermute | solution.py:142
  98.3 3.2 %collective-permute-start.10 = (f32[128,256]{1,0:T(8,128)S(1)}, f32[128,256]{1,0:T(8,128)S(1)}, u32[]{:S(2)}, u32[]{:S(2)}) collective-permute-start(f32[128,256]{1,0:T(8,128)S(1)} %add.33), channel_id=1, source_target_pairs={{0,14},{2,0},{4,2},{6,4},{8,6},{10,8},{12,10},{14,12},{1,15},{3,1}... | collective-permute-start | bytes 393224 | tf_op jit(solution)/shard_map/ppermute | solution.py:142
  101.5 0.0 collective-permute-done.13
  101.6 0.1 collective-permute-start.14
  101.7 1.7 %collective-permute-done.10 = f32[128,256]{1,0:T(8,128)S(1)} collective-permute-done((f32[128,256]{1,0:T(8,128)S(1)}, f32[128,256]{1,0:T(8,128)S(1)}, u32[]{:S(2)}, u32[]{:S(2)}) %collective-permute-start.10) | collective-permute-done | bytes 131104 | tf_op jit(solution)/shard_map/ppermute | solution.py:142
  103.4 3.5 %collective-permute-start.11 = (f32[128,256]{1,0:T(8,128)S(1)}, f32[128,256]{1,0:T(8,128)S(1)}, u32[]{:S(2)}, u32[]{:S(2)}) collective-permute-start(f32[128,256]{1,0:T(8,128)S(1)} %add.34), channel_id=1, source_target_pairs={{0,14},{2,0},{4,2},{6,4},{8,6},{10,8},{12,10},{14,12},{1,15},{3,1}... | collective-permute-start | bytes 393224 | tf_op jit(solution)/shard_map/ppermute | solution.py:142
  106.9 0.1 collective-permute-done.14
  107.0 0.7 add.38
  107.6 0.0 collective-permute-start.15
  107.6 1.8 %collective-permute-done.11 = f32[128,256]{1,0:T(8,128)S(1)} collective-permute-done((f32[128,256]{1,0:T(8,128)S(1)}, f32[128,256]{1,0:T(8,128)S(1)}, u32[]{:S(2)}, u32[]{:S(2)}) %collective-permute-start.11) | collective-permute-done | bytes 131104 | tf_op jit(solution)/shard_map/ppermute | solution.py:142
  109.4 0.7 add.35
  110.1 3.4 %collective-permute-start.12 = (f32[128,256]{1,0:T(8,128)}, f32[128,256]{1,0:T(8,128)}, u32[]{:S(2)}, u32[]{:S(2)}) collective-permute-start(f32[128,256]{1,0:T(8,128)} %add.35), channel_id=1, source_target_pairs={{0,14},{2,0},{4,2},{6,4},{8,6},{10,8},{12,10},{14,12},{1,15},{3,1}... | collective-permute-start | bytes 393224 | tf_op jit(solution)/shard_map/ppermute | solution.py:142
  113.5 0.2 copy.8
  113.7 2.0 %broadcast_in_dim.5 = f32[8,128,2,128]{3,2,1,0:T(2,128)} broadcast(f32[8,128,2]{2,1,0:T(8,128)S(1)} %copy.8), dimensions={0,1,2} | broadcast | bytes 1056768 | tf_op jit(solution)/shard_map/broadcast_in_dim | solution.py:189
  115.8 2.1 %reshape.35 = f32[8,128,256]{2,1,0:T(8,128)S(1)} reshape(f32[8,128,2,128]{3,2,1,0:T(2,128)} %broadcast_in_dim.5) | data formatting | bytes 2097152 | tf_op jit(solution)/shard_map/reshape | solution.py:189
  117.9 0.0 collective-permute-done.15
  117.9 0.0 collective-permute-done.12
  117.9 0.9 add_convert_fusion
  118.8 1.2 multiply_reduce_fusion
  120.0 0.0 all-to-all-done.3
  120.0 0.3 reduce
  120.3 7.1 %collective-permute-start.16 = (bf16[64,1024]{1,0:T(8,128)(2,1)S(1)}, bf16[64,1024]{1,0:T(8,128)(2,1)S(1)}, u32[]{:S(2)}, u32[]{:S(2)}) collective-permute-start(bf16[64,1024]{1,0:T(8,128)(2,1)S(1)} %pad_maximum_fusion), channel_id=1, source_target_pairs={{0,64},{64,0},{1,65},{65,1},{2,66},{66,2},{3,67},{67,3},{4,68},{68... | collective-permute-start | bytes 393224 | tf_op jit(solution)/shard_map/ppermute | solution.py:137
  127.4 1.0 collective-permute-done.16
  128.4 0.6 pad_maximum_fusion.9
  129.0 0.6 pad_maximum_fusion.8
  129.7 0.6 pad_maximum_fusion.7
  130.3 0.6 pad_maximum_fusion.6
  (50 shorter events, 0.3 us)
Async XLA Ops:
  1.5 4.2 %collective-permute-start.8 = (bf16[64,512]{1,0:T(8,128)(2,1)S(1)}, bf16[64,512]{1,0:T(8,128)(2,1)S(1)}, u32[]{:S(2)}, u32[]{:S(2)}) collective-permute-start(bf16[64,512]{1,0:T(8,128)(2,1)S(1)} %pad_maximum_fusion.5), channel_id=1, source_target_pairs={{0,64},{64,0},{1,65},{65,1},{2,66},{66,2},{3,67},{67,3},{4,68},{68... | collective-permute-start | bytes 196616 | tf_op jit(solution)/shard_map/ppermute | solution.py:137
  7.3 5.2 %copy-start.17 = (bf16[64,512]{1,0:T(8,128)(2,1)S(1)}, bf16[64,512]{1,0:T(8,128)(2,1)}, u32[]{:S(2)}) copy-start(bf16[64,512]{1,0:T(8,128)(2,1)} %param.7) | copy-start | bytes 196612
  7.3 5.2 %copy-start.18 = (bf16[64,512]{1,0:T(8,128)(2,1)S(1)}, bf16[64,512]{1,0:T(8,128)(2,1)}, u32[]{:S(2)}) copy-start(bf16[64,512]{1,0:T(8,128)(2,1)} %param.4) | copy-start | bytes 196612
  7.3 35.9 %all-to-all-start = ((bf16[16,128,512]{2,1,0:T(8,128)(2,1)}), bf16[16,128,512]{2,1,0:T(8,128)(2,1)S(1)}, u32[]{:S(2)}, u32[]{:S(2)}) async-start(bf16[16,128,512]{2,1,0:T(8,128)(2,1)} %broadcast_in_dim.4), calls=%async_computation | async-start | bytes 4194304 | tf_op jit(solution)/shard_map/all_to_all | solution.py:146
  12.5 1.6 %collective-permute-start = (bf16[64,512]{1,0:T(8,128)(2,1)S(1)}, bf16[64,512]{1,0:T(8,128)(2,1)S(1)}, u32[]{:S(2)}, u32[]{:S(2)}) collective-permute-start(bf16[64,512]{1,0:T(8,128)(2,1)S(1)} %pad_maximum_fusion.4), channel_id=1, source_target_pairs={{0,64},{64,0},{1,65},{65,1},{2,66},{66,2},{3,67},{67,3},{4,68},{68... | collective-permute-start | bytes 196616 | tf_op jit(solution)/shard_map/ppermute | solution.py:137
  14.1 29.0 %copy-start.3 = (bf16[128,512]{1,0:T(8,128)(2,1)}, bf16[128,512]{1,0:T(8,128)(2,1)S(1)}, u32[]{:S(2)}) copy-start(bf16[128,512]{1,0:T(8,128)(2,1)S(1)} %pad_maximum_fusion.2.refs_4_) | copy-start | bytes 393220
  14.1 9.2 %collective-permute-start.1 = (bf16[128,512]{1,0:T(8,128)(2,1)S(1)}, bf16[128,512]{1,0:T(8,128)(2,1)S(1)}, u32[]{:S(2)}, u32[]{:S(2)}) collective-permute-start(bf16[128,512]{1,0:T(8,128)(2,1)S(1)} %pad_maximum_fusion.2.refs_4_), channel_id=1, source_target_pairs={{0,2},{2,4},{4,6},{6,8},{8,10},{10,12},{12,14},{14,0},{1,3},{3,5},... | collective-permute-start | bytes 393224 | tf_op jit(solution)/shard_map/ppermute | solution.py:142
  15.9 7.5 %collective-permute-start.5 = (bf16[128,512]{1,0:T(8,128)(2,1)S(1)}, bf16[128,512]{1,0:T(8,128)(2,1)S(1)}, u32[]{:S(2)}, u32[]{:S(2)}) collective-permute-start(bf16[128,512]{1,0:T(8,128)(2,1)S(1)} %pad_maximum_fusion.2.refs_4_), channel_id=1, source_target_pairs={{0,14},{2,0},{4,2},{6,4},{8,6},{10,8},{12,10},{14,12},{1,15},{3,1}... | collective-permute-start | bytes 393224 | tf_op jit(solution)/shard_map/ppermute | solution.py:142
  23.4 19.8 %copy-start.10 = (bf16[128,512]{1,0:T(8,128)(2,1)}, bf16[128,512]{1,0:T(8,128)(2,1)S(1)}, u32[]{:S(2)}) copy-start(bf16[128,512]{1,0:T(8,128)(2,1)S(1)} %collective-permute-done.1.refs_3_) | copy-start | bytes 393220
  23.4 5.4 %collective-permute-start.2 = (bf16[128,512]{1,0:T(8,128)(2,1)S(1)}, bf16[128,512]{1,0:T(8,128)(2,1)S(1)}, u32[]{:S(2)}, u32[]{:S(2)}) collective-permute-start(bf16[128,512]{1,0:T(8,128)(2,1)S(1)} %collective-permute-done.1.refs_3_), channel_id=1, source_target_pairs={{0,2},{2,4},{4,6},{6,8},{8,10},{10,12},{12,14},{14,0},{1,3},{3,5},... | collective-permute-start | bytes 393224 | tf_op jit(solution)/shard_map/ppermute | solution.py:142
  23.4 19.8 %copy-start.11 = (bf16[128,512]{1,0:T(8,128)(2,1)}, bf16[128,512]{1,0:T(8,128)(2,1)S(1)}, u32[]{:S(2)}) copy-start(bf16[128,512]{1,0:T(8,128)(2,1)S(1)} %collective-permute-done.5.refs_5_) | copy-start | bytes 393220
  23.4 5.3 %collective-permute-start.6 = (bf16[128,512]{1,0:T(8,128)(2,1)S(1)}, bf16[128,512]{1,0:T(8,128)(2,1)S(1)}, u32[]{:S(2)}, u32[]{:S(2)}) collective-permute-start(bf16[128,512]{1,0:T(8,128)(2,1)S(1)} %collective-permute-done.5.refs_5_), channel_id=1, source_target_pairs={{0,14},{2,0},{4,2},{6,4},{8,6},{10,8},{12,10},{14,12},{1,15},{3,1}... | collective-permute-start | bytes 393224 | tf_op jit(solution)/shard_map/ppermute | solution.py:142
  28.7 14.4 %copy-start.12 = (bf16[128,512]{1,0:T(8,128)(2,1)}, bf16[128,512]{1,0:T(8,128)(2,1)S(1)}, u32[]{:S(2)}) copy-start(bf16[128,512]{1,0:T(8,128)(2,1)S(1)} %collective-permute-done.2.refs_2_) | copy-start | bytes 393220
  28.7 5.3 %collective-permute-start.3 = (bf16[128,512]{1,0:T(8,128)(2,1)S(1)}, bf16[128,512]{1,0:T(8,128)(2,1)S(1)}, u32[]{:S(2)}, u32[]{:S(2)}) collective-permute-start(bf16[128,512]{1,0:T(8,128)(2,1)S(1)} %collective-permute-done.2.refs_2_), channel_id=1, source_target_pairs={{0,2},{2,4},{4,6},{6,8},{8,10},{10,12},{12,14},{14,0},{1,3},{3,5},... | collective-permute-start | bytes 393224 | tf_op jit(solution)/shard_map/ppermute | solution.py:142
  28.8 14.4 %copy-start.13 = (bf16[128,512]{1,0:T(8,128)(2,1)}, bf16[128,512]{1,0:T(8,128)(2,1)S(1)}, u32[]{:S(2)}) copy-start(bf16[128,512]{1,0:T(8,128)(2,1)S(1)} %collective-permute-done.6.refs_6_) | copy-start | bytes 393220
  28.8 5.3 %collective-permute-start.7 = (bf16[128,512]{1,0:T(8,128)(2,1)S(1)}, bf16[128,512]{1,0:T(8,128)(2,1)S(1)}, u32[]{:S(2)}, u32[]{:S(2)}) collective-permute-start(bf16[128,512]{1,0:T(8,128)(2,1)S(1)} %collective-permute-done.6.refs_6_), channel_id=1, source_target_pairs={{0,14},{2,0},{4,2},{6,4},{8,6},{10,8},{12,10},{14,12},{1,15},{3,1}... | collective-permute-start | bytes 393224 | tf_op jit(solution)/shard_map/ppermute | solution.py:142
  34.1 9.1 %copy-start.14 = (bf16[128,512]{1,0:T(8,128)(2,1)}, bf16[128,512]{1,0:T(8,128)(2,1)S(1)}, u32[]{:S(2)}) copy-start(bf16[128,512]{1,0:T(8,128)(2,1)S(1)} %collective-permute-done.3.refs_1_) | copy-start | bytes 393220
  34.1 5.3 %collective-permute-start.4 = (bf16[128,512]{1,0:T(8,128)(2,1)S(1)}, bf16[128,512]{1,0:T(8,128)(2,1)S(1)}, u32[]{:S(2)}, u32[]{:S(2)}) collective-permute-start(bf16[128,512]{1,0:T(8,128)(2,1)S(1)} %collective-permute-done.3.refs_1_), channel_id=1, source_target_pairs={{0,2},{2,4},{4,6},{6,8},{8,10},{10,12},{12,14},{14,0},{1,3},{3,5},... | collective-permute-start | bytes 393224 | tf_op jit(solution)/shard_map/ppermute | solution.py:142
  34.1 9.1 %copy-start.15 = (bf16[128,512]{1,0:T(8,128)(2,1)}, bf16[128,512]{1,0:T(8,128)(2,1)S(1)}, u32[]{:S(2)}) copy-start(bf16[128,512]{1,0:T(8,128)(2,1)S(1)} %collective-permute-done.7.refs_7_) | copy-start | bytes 393220
  39.4 3.8 %copy-start.16 = (bf16[128,512]{1,0:T(8,128)(2,1)}, bf16[128,512]{1,0:T(8,128)(2,1)S(1)}, u32[]{:S(2)}) copy-start(bf16[128,512]{1,0:T(8,128)(2,1)S(1)} %collective-permute-done.4.refs_0_) | copy-start | bytes 393220
  43.2 1.4 %copy-start = (bf16[16,128,512]{2,1,0:T(8,128)(2,1)}, bf16[16,128,512]{2,1,0:T(8,128)(2,1)S(1)}, u32[]{:S(2)}) copy-start(bf16[16,128,512]{2,1,0:T(8,128)(2,1)S(1)} %all-to-all-done) | copy-start | bytes 6291460
  71.0 18.3 %all-to-all-start.1 = ((bf16[8,128,256]{2,1,0:T(8,128)(2,1)}), bf16[8,128,256]{2,1,0:T(8,128)(2,1)S(1)}, u32[]{:S(2)}, u32[]{:S(2)}) async-start(bf16[8,128,256]{2,1,0:T(8,128)(2,1)} %bitcast.9), calls=%async_computation.1 | async-start | bytes 1048576 | tf_op jit(solution)/shard_map/all_to_all | solution.py:146
  89.3 0.8 copy-start.1
  89.3 4.5 %copy-start.20 = (f32[128,256]{1,0:T(8,128)S(1)}, f32[128,256]{1,0:T(8,128)}, u32[]{:S(2)}) copy-start(f32[128,256]{1,0:T(8,128)} %get-tuple-element.20) | copy-start | bytes 393220
  89.3 7.0 %copy-start.19 = (f32[128,256]{1,0:T(8,128)S(1)}, f32[128,256]{1,0:T(8,128)}, u32[]{:S(2)}) copy-start(f32[128,256]{1,0:T(8,128)} %get-tuple-element.24) | copy-start | bytes 393220
  89.3 8.9 %copy-start.9 = (f32[128,256]{1,0:T(8,128)S(1)}, f32[128,256]{1,0:T(8,128)}, u32[]{:S(2)}) copy-start(f32[128,256]{1,0:T(8,128)} %get-tuple-element.21) | copy-start | bytes 393220
  89.3 12.1 %copy-start.2 = (f32[8,4,1024]{2,1,0:T(4,128)S(1)}, f32[8,4,1024]{2,1,0:T(4,128)}, u32[]{:S(2)}) copy-start(f32[8,4,1024]{2,1,0:T(4,128)} %all_to_all.20.stats_ref) | copy-start | bytes 393220
  89.3 12.2 %copy-start.8 = (f32[128,256]{1,0:T(8,128)S(1)}, f32[128,256]{1,0:T(8,128)}, u32[]{:S(2)}) copy-start(f32[128,256]{1,0:T(8,128)} %get-tuple-element.25) | copy-start | bytes 393220
  89.4 14.0 %copy-start.7 = (f32[128,256]{1,0:T(8,128)S(1)}, f32[128,256]{1,0:T(8,128)}, u32[]{:S(2)}) copy-start(f32[128,256]{1,0:T(8,128)} %get-tuple-element.22) | copy-start | bytes 393220
  89.4 17.6 %copy-start.6 = (f32[128,256]{1,0:T(8,128)S(1)}, f32[128,256]{1,0:T(8,128)}, u32[]{:S(2)}) copy-start(f32[128,256]{1,0:T(8,128)} %get-tuple-element.26) | copy-start | bytes 393220
  89.4 20.0 %copy-start.5 = (f32[128,256]{1,0:T(8,128)S(1)}, f32[128,256]{1,0:T(8,128)}, u32[]{:S(2)}) copy-start(f32[128,256]{1,0:T(8,128)} %get-tuple-element.23) | copy-start | bytes 393220
  90.1 29.9 %all-to-all-start.3 = ((bf16[16,128,512]{2,1,0:T(8,128)(2,1)}), bf16[16,128,512]{2,1,0:T(8,128)(2,1)S(1)}, u32[]{:S(2)}, u32[]{:S(2)}) async-start(bf16[16,128,512]{2,1,0:T(8,128)(2,1)} %bitcast.8), calls=%async_computation.3 | async-start | bytes 4194304 | tf_op jit(solution)/shard_map/all_to_all | solution.py:146
  93.8 4.4 %collective-permute-start.9 = (f32[128,256]{1,0:T(8,128)S(1)}, f32[128,256]{1,0:T(8,128)S(1)}, u32[]{:S(2)}, u32[]{:S(2)}) collective-permute-start(f32[128,256]{1,0:T(8,128)S(1)} %copy-done.20), channel_id=1, source_target_pairs={{0,14},{2,0},{4,2},{6,4},{8,6},{10,8},{12,10},{14,12},{1,15},{3,1}... | collective-permute-start | bytes 393224 | tf_op jit(solution)/shard_map/ppermute | solution.py:142
  96.3 5.2 %collective-permute-start.13 = (f32[128,256]{1,0:T(8,128)S(1)}, f32[128,256]{1,0:T(8,128)S(1)}, u32[]{:S(2)}, u32[]{:S(2)}) collective-permute-start(f32[128,256]{1,0:T(8,128)S(1)} %copy-done.19), channel_id=1, source_target_pairs={{0,2},{2,4},{4,6},{6,8},{8,10},{10,12},{12,14},{14,0},{1,3},{3,5},... | collective-permute-start | bytes 393224 | tf_op jit(solution)/shard_map/ppermute | solution.py:142
  98.3 5.1 %collective-permute-start.10 = (f32[128,256]{1,0:T(8,128)S(1)}, f32[128,256]{1,0:T(8,128)S(1)}, u32[]{:S(2)}, u32[]{:S(2)}) collective-permute-start(f32[128,256]{1,0:T(8,128)S(1)} %add.33), channel_id=1, source_target_pairs={{0,14},{2,0},{4,2},{6,4},{8,6},{10,8},{12,10},{14,12},{1,15},{3,1}... | collective-permute-start | bytes 393224 | tf_op jit(solution)/shard_map/ppermute | solution.py:142
  101.6 5.4 %collective-permute-start.14 = (f32[128,256]{1,0:T(8,128)S(1)}, f32[128,256]{1,0:T(8,128)S(1)}, u32[]{:S(2)}, u32[]{:S(2)}) collective-permute-start(f32[128,256]{1,0:T(8,128)S(1)} %add.37), channel_id=1, source_target_pairs={{0,2},{2,4},{4,6},{6,8},{8,10},{10,12},{12,14},{14,0},{1,3},{3,5},... | collective-permute-start | bytes 393224 | tf_op jit(solution)/shard_map/ppermute | solution.py:142
  103.4 6.0 %collective-permute-start.11 = (f32[128,256]{1,0:T(8,128)S(1)}, f32[128,256]{1,0:T(8,128)S(1)}, u32[]{:S(2)}, u32[]{:S(2)}) collective-permute-start(f32[128,256]{1,0:T(8,128)S(1)} %add.34), channel_id=1, source_target_pairs={{0,14},{2,0},{4,2},{6,4},{8,6},{10,8},{12,10},{14,12},{1,15},{3,1}... | collective-permute-start | bytes 393224 | tf_op jit(solution)/shard_map/ppermute | solution.py:142
  107.6 10.2 %collective-permute-start.15 = (f32[128,256]{1,0:T(8,128)}, f32[128,256]{1,0:T(8,128)S(1)}, u32[]{:S(2)}, u32[]{:S(2)}) collective-permute-start(f32[128,256]{1,0:T(8,128)} %add.38), channel_id=1, source_target_pairs={{0,2},{2,4},{4,6},{6,8},{8,10},{10,12},{12,14},{14,0},{1,3},{3,5},... | collective-permute-start | bytes 393224 | tf_op jit(solution)/shard_map/ppermute | solution.py:142
  110.1 7.8 %collective-permute-start.12 = (f32[128,256]{1,0:T(8,128)}, f32[128,256]{1,0:T(8,128)}, u32[]{:S(2)}, u32[]{:S(2)}) collective-permute-start(f32[128,256]{1,0:T(8,128)} %add.35), channel_id=1, source_target_pairs={{0,14},{2,0},{4,2},{6,4},{8,6},{10,8},{12,10},{14,12},{1,15},{3,1}... | collective-permute-start | bytes 393224 | tf_op jit(solution)/shard_map/ppermute | solution.py:142
  113.5 4.4 %copy-start.4 = (f32[128,256]{1,0:T(8,128)S(1)}, f32[128,256]{1,0:T(8,128)}, u32[]{:S(2)}) copy-start(f32[128,256]{1,0:T(8,128)} %get-tuple-element.19) | copy-start | bytes 393220
  120.3 8.1 %collective-permute-start.16 = (bf16[64,1024]{1,0:T(8,128)(2,1)S(1)}, bf16[64,1024]{1,0:T(8,128)(2,1)S(1)}, u32[]{:S(2)}, u32[]{:S(2)}) collective-permute-start(bf16[64,1024]{1,0:T(8,128)(2,1)S(1)} %pad_maximum_fusion), channel_id=1, source_target_pairs={{0,64},{64,0},{1,65},{65,1},{2,66},{66,2},{3,67},{67,3},{4,68},{68... | collective-permute-start | bytes 393224 | tf_op jit(solution)/shard_map/ppermute | solution.py:137

commit v3 on v2

v3 whole, which is shorter than its diff:
```python
import functools
import math

import jax
import jax.numpy as jnp
from jax import lax
from jax.experimental import pallas as pl
from jax.experimental.pallas import tpu as pltpu
from jax.sharding import Mesh, PartitionSpec as P

DH = 128
PAIR = 2 * DH
SCALING = 1.0 / math.sqrt(DH)
SCALING2 = SCALING * math.log2(math.e)
F32 = jnp.float32
BF16 = jnp.bfloat16
LINE = "z"
PLANE = ("yh", "x", "yl")
TOKENS = P(("x", "z", "yl", "yh", "c"), None)
FORWARD_VMEM, BACKWARD_VMEM = 24 << 20, 32 << 20
IN_VMEM = pl.BlockSpec(memory_space=pltpu.VMEM)
IN_SMEM = pl.BlockSpec(memory_space=pltpu.SMEM)


def dot(a, b, ca, cb):
    return lax.dot_general(a, b, (((ca,), (cb,)), ((), ())), preferred_element_type=F32)


def in_line(z, step, size, width):
    return pl.ds(pl.multiple_of(lax.rem(z + (step + size), size) * width, width), width)


def rows_of(pieces, columns):
    return jnp.concatenate([p[:, columns] for p in pieces], 0)


FIRST, SECOND = slice(0, DH), slice(DH, PAIR)


def forward_kernel(count, *refs):
    pieces, refs = refs[: 2 * count], refs[2 * count :]
    kv_ref, outs, tops, stats_ref = refs[0], refs[1 : count + 1], refs[count + 1 : -1], refs[-1]
    values_t = kv_ref[:, SECOND].T
    for n in range(count):
        rows = pieces[2 * n : 2 * n + 2]
        scores = dot(kv_ref[:, FIRST], rows_of(rows, FIRST), 1, 1)
        top = jnp.max(scores, axis=0, keepdims=True)
        exp = jnp.exp2((scores - top) * SCALING2)
        total = jnp.sum(exp, axis=0, keepdims=True)
        out_t = dot(values_t, exp.astype(BF16), 1, 0)
        outs[n][...] = out_t
        tops[n][...] = top * SCALING2
        here = slice(n * out_t.shape[1], (n + 1) * out_t.shape[1])
        stats_ref[0:1, here] = top * SCALING2 + jnp.log2(total)
        stats_ref[1:2, here] = (
            jnp.sum(rows_of(rows, SECOND).T.astype(F32) * out_t, axis=0, keepdims=True) / total
        )


def forward(pieces, kv):
    count, width = len(pieces) // 2, 2 * pieces[0].shape[0]
    got = pl.pallas_call(
        functools.partial(forward_kernel, count),
        in_specs=[IN_VMEM] * (len(pieces) + 1),
        out_specs=[IN_VMEM] * (2 * count + 1),
        out_shape=[jax.ShapeDtypeStruct((n, width), F32) for n in (DH, 1) for _ in range(count)]
        + [jax.ShapeDtypeStruct((2, count * width), F32)],
        compiler_params=pltpu.CompilerParams(vmem_limit_bytes=FORWARD_VMEM),
        name="forward",
    )(*pieces, kv)
    return [got[n : 2 * count : count] for n in range(count)], got[-1]


def backward_kernel(steps, carried, last, size, z_ref, *refs):
    count = len(steps)
    pieces, refs = refs[:count], refs[count:]
    saved, refs = refs[:count], refs[count:]
    stats_ref, kv_ref, refs = refs[0], refs[1], refs[2:]
    if carried:
        start_ref, refs = refs[0], refs[1:]
    grads, dkv_ref, merged_ref = refs[:count], refs[count], refs[-1]
    sum_ref = refs[count + 1] if last else dkv_ref
    width = pieces[0].shape[0]
    z = z_ref[0]
    logs = [stats_ref[j, 0:1, :] for j in range(size)]
    top = functools.reduce(jnp.maximum, logs)
    log_total = top + jnp.log2(sum(jnp.exp2(x - top) for x in logs))
    merged_ref[0:1, :] = log_total
    merged_ref[1:2, :] = sum(jnp.exp2(x - log_total) * stats_ref[j, 1:2, :] for j, x in enumerate(logs))
    keys_t = kv_ref[:, FIRST].T
    for n in range(count // 2):
        rows = pieces[2 * n : 2 * n + 2]
        out_ref, top_ref = saved[2 * n : 2 * n + 2]
        where = [in_line(z, step, size, width) for step in steps[2 * n : 2 * n + 2]]
        log_total, delta = [jnp.concatenate([merged_ref[k : k + 1, w] for w in where], 1) for k in range(2)]
        share = jnp.exp2(top_ref[...] - log_total)
        scores = dot(kv_ref[:, FIRST], rows_of(rows, FIRST), 1, 1)
        weights = jnp.exp2(scores * SCALING2 - log_total)
        upstream_dot = dot(kv_ref[:, SECOND], rows_of(rows, SECOND), 1, 1)
        score_grad = (weights * (upstream_dot - delta)).astype(BF16)
        dv = dot(weights.astype(BF16), rows_of(rows, SECOND), 1, 0)
        dk = dot(score_grad, rows_of(rows, FIRST), 1, 0) * SCALING
        if n == 0 and not carried:
            sum_ref[:, FIRST] = dk
            sum_ref[:, SECOND] = dv
        else:
            before = start_ref if n == 0 else sum_ref
            sum_ref[:, FIRST] = before[:, FIRST] + dk
            sum_ref[:, SECOND] = before[:, SECOND] + dv
        dq_t = dot(keys_t, score_grad, 1, 0) * SCALING
        out_t = out_ref[...] * share
        for k in range(2):
            here = slice(k * width, (k + 1) * width)
            grads[2 * n + k][:, FIRST] = out_t[:, here].T.astype(BF16)
            grads[2 * n + k][:, SECOND] = dq_t[:, here].T.astype(BF16)
    if last:
        high = sum_ref[...].astype(BF16)
        dkv_ref[:, :PAIR] = high
        dkv_ref[:, PAIR:] = (sum_ref[:, FIRST] - high[:, FIRST].astype(F32)).astype(BF16)


def backward(z, steps, pieces, saved, stats, kv, carried, last):
    size, _, nq = stats.shape
    nk, width = kv.shape[0], pieces[0].shape[0]
    got = pl.pallas_call(
        functools.partial(backward_kernel, steps, len(carried), last, size),
        in_specs=[IN_SMEM] + [IN_VMEM] * (len(pieces) + len(saved) + 2 + len(carried)),
        out_specs=[IN_VMEM] * (len(steps) + 1),
        out_shape=[jax.ShapeDtypeStruct((width, PAIR), BF16)] * len(steps)
        + [jax.ShapeDtypeStruct((nk, 3 * DH), BF16) if last else jax.ShapeDtypeStruct((nk, PAIR), F32)],
        scratch_shapes=[pltpu.VMEM((nk, PAIR), F32)] * last + [pltpu.VMEM((2, nq), F32)],
        compiler_params=pltpu.CompilerParams(vmem_limit_bytes=BACKWARD_VMEM),
        name="backward",
    )(z, *pieces, *saved, stats, kv, *carried)
    return dict(zip(steps, got[:-1])), got[-1]


def join_kernel(core_ref, kept_ref, away_ref, *out_refs):
    first = core_ref[0] == 0
    for n, ref in enumerate(out_refs):
        here = slice(n * PAIR, (n + 1) * PAIR)
        a, b = kept_ref[:, here], away_ref[:, here]
        ref[:, :PAIR] = jnp.where(first, a, b)
        ref[:, PAIR:] = jnp.where(first, b, a)


def join_heads(core, kept, away):
    shape = jax.ShapeDtypeStruct((kept.shape[0], 2 * PAIR), BF16)
    return pl.pallas_call(
        join_kernel,
        in_specs=[IN_SMEM] + [IN_VMEM] * 2,
        out_specs=[IN_VMEM] * 4,
        out_shape=[shape] * 4,
        compiler_params=pltpu.CompilerParams(vmem_limit_bytes=4 << 20),
        name="join_heads",
    )(core, kept, away)


def swapped(x, axis):
    return lax.ppermute(x, axis, [(0, 1), (1, 0)])


def along_line(x, by):
    size = lax.axis_size(LINE)
    return lax.ppermute(x, LINE, [(i, (i + by) % size) for i in range(size)])


def along_line_and_across(x, by):
    size = lax.axis_size(LINE)
    pairs = [(2 * i + j, 2 * ((i + by) % size) + 1 - j) for i in range(size) for j in range(2)]
    return lax.ppermute(x, (LINE, "yl"), pairs)


def exchange(x, axes):
    return lax.all_to_all(x, axes, split_axis=0, concat_axis=0, tiled=True)


def add(a, b):
    return (a.astype(F32) + b.astype(F32)).astype(BF16)


def split(which, *arrays):
    halves = [(x[:, : x.shape[1] // 2], x[:, x.shape[1] // 2 :]) for x in arrays]
    kept = [jnp.where(which == 0, a, b) for a, b in halves]
    sent = [jnp.where(which == 0, b, a) for a, b in halves]
    return jnp.concatenate(kept, 1), jnp.concatenate(sent, 1)


def joined(which, mine, other):
    return jnp.concatenate([jnp.where(which == 0, mine, other), jnp.where(which == 0, other, mine)], 1)


def shards(queries, keys, values, upstream):
    core, low = lax.axis_index("c"), lax.axis_index("yl")
    core1 = core.astype(jnp.int32).reshape(1)
    z = lax.axis_index(LINE).astype(jnp.int32).reshape(1)
    line, plane = lax.axis_size(LINE), lax.axis_size(PLANE)
    rows = queries.shape[0]

    kept_kv, sent_kv = split(core, keys, values)
    kept, sent = split(core, queries, upstream)
    qg = jnp.concatenate([kept, swapped(sent, "c")], 0)
    kept, sent = split(low, qg[:, :PAIR], qg[:, PAIR:])
    pieces = {0: jnp.concatenate([kept, swapped(sent, "yl")], 0)}
    sent_kv, qg = lax.optimization_barrier((sent_kv, qg))
    kv = jnp.concatenate([kept_kv, swapped(sent_kv, "c")], 0)
    kv = jnp.stack([jnp.concatenate([kv[:, i : i + DH], kv[:, PAIR + i : PAIR + i + DH]], 1) for i in (0, DH)])
    kv = jnp.broadcast_to(kv[None], (plane // 2,) + kv.shape).reshape((plane,) + kv.shape[1:])
    kv = exchange(kv, PLANE).reshape(-1, PAIR)

    for step in range(1, line // 2 + 1):
        pieces[-step] = along_line(pieces[1 - step], 1)
        if step < line // 2:
            pieces[step] = along_line(pieces[step - 1], -1)
    groups = [[0, -1, 1, -2], [2, -3], [3, -4]]
    steps = sum(groups, [])
    parts = [forward([pieces[s] for s in group], kv) for group in groups]
    stats = jnp.concatenate([p[1] for p in parts], 1).reshape(2, line, 4 * rows)
    saved = dict(zip(steps[::2], sum([p[0] for p in parts], [])))
    source = jnp.argsort(jnp.array(steps) % line)
    stats = jnp.take(stats, source[(jnp.arange(line) - z) % line], axis=1).reshape(1, 2, -1)
    stats = exchange(jnp.broadcast_to(stats, (line,) + stats.shape[1:]), LINE)

    def backward_of(group, carried, last):
        kept = [x for s in group[::2] for x in saved[s]]
        return backward(z, group, [pieces[s] for s in group], kept, stats, kv, carried, last)

    grads, dkv_part = backward_of([3, -4], (), False)
    up, down = along_line(grads[-4], -1), along_line(grads[3], 1)
    more, dkv_part = backward_of([2, -3, 1, -2], (dkv_part,), False)
    grads.update(more)
    dkv_part, up, down = lax.optimization_barrier((dkv_part, up, down))
    up, down = along_line(add(up, grads[-3]), -1), along_line(add(down, grads[2]), 1)
    more, dkv_part = backward_of([0, -1], (dkv_part,), True)
    grads.update(more)
    dkv_parts = exchange(dkv_part.reshape(plane, -1, 3 * DH), PLANE)
    up, down = along_line(add(up, grads[-2]), -1), along_line(add(down, grads[1]), 1)
    near = 2 * rows
    up = add(up, grads[-1])
    own = add(down, grads[0])
    mine = add(along_line(up[:near], -1), own[:near])
    other = add(along_line_and_across(up[near:], -1), swapped(own[near:], "yl"))
    dkv = jnp.sum(dkv_parts.astype(F32).reshape(plane // 2, 2, 2 * rows, 3 * DH), axis=0)
    dkv = jnp.concatenate([dkv[:, :, :DH] + dkv[:, :, PAIR:], dkv[:, :, DH:PAIR]], 2).astype(BF16)
    results = jnp.concatenate(
        [joined(low, mine[:, FIRST], other[:, FIRST]), joined(low, mine[:, SECOND], other[:, SECOND])]
        + [dkv[i, :, columns] for columns in (FIRST, SECOND) for i in (0, 1)],
        1,
    )
    kept, away = results[:rows], swapped(results[rows:], "c")
    return tuple(join_heads(core1, kept, away))


def solution(mesh):
    fine = Mesh(mesh.devices.reshape(2, 2, 4, 8, 2), ("yh", "c", "x", "z", "yl"))
    return jax.shard_map(
        shards, mesh=fine, in_specs=(TOKENS,) * 4, out_specs=(TOKENS,) * 4, check_vma=False
    )
```

time: 132 us -> 104 us (0.79)
  waiting for transfers between devices: 26.2 us -> 18.3 us
  Pallas kernels: 24.8 us -> 19 us
  local copies, waits for them, and re-layouts: 7.98 us -> 2.55 us
  other arithmetic: 7.27 us -> 3.85 us
  blocking collectives: 16.2 us -> 13.6 us
  starting transfers between devices: 47.4 us -> 45.6 us
    ppermute x14, waiting for transfers between devices: 19.7 us -> 10.7 us  [along_line(): return lax.ppermute(x, LINE, [(i, (i + by) % size) for i in range(size)])]
    pallas_call x2 -> x7, Pallas kernels: 24.8 us -> 19 us  [the longest x3 11.9 us: backward(): pl.pallas_call(functools.partial(backward_kernel, steps, len(carried), la...]
    ppermute x3 -> x6, waiting for transfers between devices: 2.79 us -> 7.57 us  [the longest x5 4.26 us: swapped(): return lax.ppermute(x, axis, [(0, 1), (1, 0)])]
    all_to_all x3 -> x2, waiting for transfers between devices: 3.78 us -> 0.01 us  [exchange(): return lax.all_to_all(x, axes, split_axis=0, concat_axis=0, tiled=True)]
    all_to_all x1, blocking collectives: 16.2 us -> 13.6 us  [exchange(): return lax.all_to_all(x, axes, split_axis=0, concat_axis=0, tiled=True)]
    ppermute x14, starting transfers between devices: 23.7 us -> 21.2 us  [along_line(): return lax.ppermute(x, LINE, [(i, (i + by) % size) for i in range(size)])]
    concatenate x9 -> x7, other arithmetic: 2.58 us -> 0.07 us  [the longest x3 0.02 us: split(): return (jnp.concatenate(kept, 1), jnp.concatenate(sent, 1))]
    broadcast_in_dim x2 -> x4, local copies, waits for them, and re-layouts: 3.6 us -> 1.21 us  [the longest x1 1.09 us: shards(): jnp.broadcast_to(kv[None], (plane // 2,) + kv.shape)]
  transfers between devices with their start and end apart: 20 -> 22, of which waited for: 12 -> 11; matrix products, arithmetic and copies ran while one was open for 6% -> 3% of each run, Pallas kernels for 11% -> 10%
where the time goes in v3:
time: 104 us
  starting transfers between devices  45.6 us (44%)
  Pallas kernels  19 us (18%)
  waiting for transfers between devices  18.3 us (18%)
  blocking collectives  13.6 us (13%)
  other arithmetic  3.85 us (4%)
  local copies, waits for them, and re-layouts  2.55 us (2%)
    ppermute x14, starting transfers between devices, along_line(): return lax.ppermute(x, LINE, [(i, (i + by) % size) for i in range(size)])  21.2 us
    all_to_all x1, blocking collectives, exchange(): return lax.all_to_all(x, axes, split_axis=0, concat_axis=0, tiled=True)  13.6 us
    ppermute x5, starting transfers between devices, swapped(): return lax.ppermute(x, axis, [(0, 1), (1, 0)])  12.3 us
    pallas_call x3, Pallas kernels, backward(): pl.pallas_call(functools.partial(backward_kernel, steps, len(carried), la...  11.9 us
    all_to_all x2, starting transfers between devices, exchange(): return lax.all_to_all(x, axes, split_axis=0, concat_axis=0, tiled=True)  11 us
    ppermute x14, waiting for transfers between devices, along_line(): return lax.ppermute(x, LINE, [(i, (i + by) % size) for i in range(size)])  10.7 us
    pallas_call x3, Pallas kernels, forward(): pl.pallas_call(functools.partial(forward_kernel, count), in_specs=[IN_VME...  6.43 us
    ppermute x5, waiting for transfers between devices, swapped(): return lax.ppermute(x, axis, [(0, 1), (1, 0)])  4.26 us
  transfers between devices with their start and end apart: 22, of which 11 were waited for; matrix products, arithmetic and copies ran while one was open for 3% of the time, Pallas kernels for 10%

profile of v3, /device:TPU:1, one launch (start us, length us, event | category | flops | bytes accessed | tf_op | source)
XLA Modules:
  0.0 104.0 jit_solution(17955975522128597323)
XLA Ops:
  0.6 0.8 broadcast_select_fusion.6
  1.5 3.3 %collective-permute-start = (bf16[64,512]{1,0:T(8,128)(2,1)S(1)}, bf16[64,512]{1,0:T(8,128)(2,1)S(1)}, u32[]{:S(2)}, u32[]{:S(2)}) collective-permute-start(bf16[64,512]{1,0:T(8,128)(2,1)S(1)} %pad_maximum_fusion.4), channel_id=1, source_target_pairs={{0,64},{64,0},{1,65},{65,1},{2,66},{66,2},{3,67},{67,3},{4,68},{68... | collective-permute-start | bytes 196616 | tf_op jit(solution)/shard_map/ppermute | solution.py:160
  4.8 0.8 broadcast_select_fusion.2
  5.6 0.1 collective-permute-done
  5.7 0.4 collective-permute-start.7
  6.2 0.1 collective-permute-start.1
  6.3 0.8 collective-permute-done.7
  7.1 0.0 copy-start
  7.2 1.1 %broadcast_in_dim.26 = bf16[8,2,128,256]{3,2,1,0:T(8,128)(2,1)} broadcast(bf16[2,128,256]{2,1,0:T(8,128)(2,1)S(1)} %pad_maximum_fusion.3), dimensions={1,2,3} | broadcast | bytes 1179648 | tf_op jit(solution)/shard_map/broadcast_in_dim | solution.py:208
  8.3 5.2 %all-to-all-start = ((bf16[16,128,256]{2,1,0:T(8,128)(2,1)}), bf16[16,128,256]{2,1,0:T(8,128)(2,1)S(1)}, u32[]{:S(2)}, u32[]{:S(2)}) async-start(bf16[16,128,256]{2,1,0:T(8,128)(2,1)} %bitcast.4), calls=%async_computation | async-start | bytes 2097152 | tf_op jit(solution)/shard_map/all_to_all | solution.py:175
  13.5 0.0 collective-permute-done.1
  13.6 1.7 %collective-permute-start.4 = (bf16[256,256]{1,0:T(8,128)(2,1)S(1)}, bf16[256,256]{1,0:T(8,128)(2,1)S(1)}, u32[]{:S(2)}, u32[]{:S(2)}) collective-permute-start(bf16[256,256]{1,0:T(8,128)(2,1)S(1)} %pad_maximum_fusion.1.refs_0_), channel_id=1, source_target_pairs={{0,2},{2,4},{4,6},{6,8},{8,10},{10,12},{12,14},{14,0},{1,3},{3,5},... | collective-permute-start | bytes 393224 | tf_op jit(solution)/shard_map/ppermute | solution.py:165
  15.3 4.0 %collective-permute-start.2 = (bf16[256,256]{1,0:T(8,128)(2,1)S(1)}, bf16[256,256]{1,0:T(8,128)(2,1)S(1)}, u32[]{:S(2)}, u32[]{:S(2)}) collective-permute-start(bf16[256,256]{1,0:T(8,128)(2,1)S(1)} %pad_maximum_fusion.1.refs_0_), channel_id=1, source_target_pairs={{0,14},{2,0},{4,2},{6,4},{8,6},{10,8},{12,10},{14,12},{1,15},{3,1}... | collective-permute-start | bytes 393224 | tf_op jit(solution)/shard_map/ppermute | solution.py:165
  19.3 3.1 %collective-permute-done.4.refs_1_ = bf16[256,256]{1,0:T(8,128)(2,1)S(1)} collective-permute-done((bf16[256,256]{1,0:T(8,128)(2,1)S(1)}, bf16[256,256]{1,0:T(8,128)(2,1)S(1)}, u32[]{:S(2)}, u32[]{:S(2)}) %collective-permute-start.4) | collective-permute-done | bytes 131104 | tf_op jit(solution)/shard_map/ppermute | solution.py:165
  22.4 0.0 collective-permute-start.5
  22.4 0.0 copy-done
  22.4 0.6 gather_fusion
  23.1 0.0 collective-permute-done.2.refs_2_
  23.1 2.7 %collective-permute-start.3 = (bf16[256,256]{1,0:T(8,128)(2,1)S(1)}, bf16[256,256]{1,0:T(8,128)(2,1)S(1)}, u32[]{:S(2)}, u32[]{:S(2)}) collective-permute-start(bf16[256,256]{1,0:T(8,128)(2,1)S(1)} %collective-permute-done.2.refs_2_), channel_id=1, source_target_pairs={{0,14},{2,0},{4,2},{6,4},{8,6},{10,8},{12,10},{14,12},{1,15},{3,1}... | collective-permute-start | bytes 393224 | tf_op jit(solution)/shard_map/ppermute | solution.py:165
  25.8 1.9 %collective-permute-done.5.refs_3_ = bf16[256,256]{1,0:T(8,128)(2,1)S(1)} collective-permute-done((bf16[256,256]{1,0:T(8,128)(2,1)S(1)}, bf16[256,256]{1,0:T(8,128)(2,1)S(1)}, u32[]{:S(2)}, u32[]{:S(2)}) %collective-permute-start.5) | collective-permute-done | bytes 131104 | tf_op jit(solution)/shard_map/ppermute | solution.py:165
  27.7 0.0 collective-permute-start.6
  27.7 0.0 collective-permute-done.3.refs_0_
  27.8 3.4 %collective-permute-start.8 = (bf16[256,256]{1,0:T(8,128)(2,1)S(1)}, bf16[256,256]{1,0:T(8,128)(2,1)S(1)}, u32[]{:S(2)}, u32[]{:S(2)}) collective-permute-start(bf16[256,256]{1,0:T(8,128)(2,1)S(1)} %collective-permute-done.3.refs_0_), channel_id=1, source_target_pairs={{0,14},{2,0},{4,2},{6,4},{8,6},{10,8},{12,10},{14,12},{1,15},{3,1}... | collective-permute-start | bytes 393224 | tf_op jit(solution)/shard_map/ppermute | solution.py:165
  31.1 1.6 %collective-permute-done.6.refs_1_ = bf16[256,256]{1,0:T(8,128)(2,1)S(1)} collective-permute-done((bf16[256,256]{1,0:T(8,128)(2,1)S(1)}, bf16[256,256]{1,0:T(8,128)(2,1)S(1)}, u32[]{:S(2)}, u32[]{:S(2)}) %collective-permute-start.6) | collective-permute-done | bytes 131104 | tf_op jit(solution)/shard_map/ppermute | solution.py:165
  32.7 0.0 collective-permute-start.9
  32.7 0.1 broadcast_in_dim.27
  32.8 0.0 all-to-all-done
  32.9 1.6 %forward.3 = (f32[128,512]{1,0:T(8,128)S(1)}, f32[1,512]{1,0:T(1,128)S(1)}, f32[2,512]{1,0:T(2,128)S(1)}) custom-call(bf16[256,256]{1,0:T(8,128)(2,1)S(1)} %collective-permute-done.3.refs_0_, bf16[256,256]{1,0:T(8,128)(2,1)S(1)} %collective-permute-done.6.refs_1_, bf16[2048,256]{1,0:T(8,128)(2,1)S(1)} %bitcast.37), custom_call_target="tpu_custom_call" | custom-call | tf_op jit(solution)/shard_map/forward/pallas_call | solution.py:62
  34.5 3.1 %forward.4 = (f32[128,512]{1,0:T(8,128)S(1)}, f32[128,512]{1,0:T(8,128)S(1)}, f32[1,512]{1,0:T(1,128)S(1)}, f32[1,512]{1,0:T(1,128)S(1)}, f32[2,1024]{1,0:T(2,128)S(1)}) custom-call(bf16[256,256]{1,0:T(8,128)(2,1)S(1)} %pad_maximum_fusion.1.refs_0_, bf16[256,256]{1,0:T(8,128)(2,1)S(1)} %collective-permute-done.4.refs_1_, ...), custom_call_target="tpu_custom_call" | custom-call | tf_op jit(solution)/shard_map/forward/pallas_call | solution.py:62
  37.7 0.0 collective-permute-done.8.refs_0_
  37.7 0.1 collective-permute-done.9.refs_1_
  37.8 1.6 %forward.5 = (f32[128,512]{1,0:T(8,128)S(1)}, f32[1,512]{1,0:T(1,128)S(1)}, f32[2,512]{1,0:T(2,128)S(1)}) custom-call(bf16[256,256]{1,0:T(8,128)(2,1)S(1)} %collective-permute-done.8.refs_0_, bf16[256,256]{1,0:T(8,128)(2,1)S(1)} %collective-permute-done.9.refs_1_, bf16[2048,256]{1,0:T(8,128)(2,1)S(1)} %bitcast.39), custom_call_target="tpu_custom_call" | custom-call | tf_op jit(solution)/shard_map/forward/pallas_call | solution.py:62
  39.4 0.6 gather_fusion.1
  40.1 13.6 %all_to_all.15.refs_4_.refs_8_ = f32[8,2,2048]{2,1,0:T(2,128)S(1)} all-to-all(f32[8,2,2048]{2,1,0:T(2,128)S(1)} %broadcast_in_dim.31), channel_id=1, replica_groups=mesh['yh'=2,'c'=2,'x'=4,'z'=8,'yl'=2] {'z'}, dimensions={0} | all-to-all | bytes 262144 | tf_op jit(solution)/shard_map/all_to_all | solution.py:175
  53.7 2.7 %backward.3 = (bf16[256,256]{1,0:T(8,128)(2,1)S(1)}, bf16[256,256]{1,0:T(8,128)(2,1)S(1)}, f32[2048,256]{1,0:T(8,128)S(1)}) custom-call(s32[1]{0:T(128)} %bitcast.1.z_ref, bf16[256,256]{1,0:T(8,128)(2,1)S(1)} %collective-permute-done.8.refs_0_, bf16[256,256]{1,0:T(8,128)(2,1)S(1)} %collective-permute-done.9.refs_1_, ...), custom_call_target="tpu_custom_call" | custom-call | tf_op jit(solution)/shard_map/backward/pallas_call | solution.py:125
  56.4 0.1 collective-permute-start.10
  56.5 1.5 %collective-permute-start.11 = (bf16[256,256]{1,0:T(8,128)(2,1)S(1)}, bf16[256,256]{1,0:T(8,128)(2,1)S(1)}, u32[]{:S(2)}, u32[]{:S(2)}) collective-permute-start(bf16[256,256]{1,0:T(8,128)(2,1)S(1)} %get-tuple-element.45), channel_id=1, source_target_pairs={{0,2},{2,4},{4,6},{6,8},{8,10},{10,12},{12,14},{14,0},{1,3},{3,5},... | collective-permute-start | bytes 393224 | tf_op jit(solution)/shard_map/ppermute | solution.py:165
  58.0 5.3 %backward.4 = (bf16[256,256]{1,0:T(8,128)(2,1)S(1)}, bf16[256,256]{1,0:T(8,128)(2,1)S(1)}, bf16[256,256]{1,0:T(8,128)(2,1)S(1)}, bf16[256,256]{1,0:T(8,128)(2,1)S(1)}, f32[2048,256]{1,0:T(8,128)S(1)}) custom-call(s32[1]{0:T(128)} %bitcast.1.z_ref, bf16[256,256]{1,0:T(8,128)(2,1)S(1)} %collective-permute-done.3.refs_0_, ...), custom_call_target="tpu_custom_call" | custom-call | tf_op jit(solution)/shard_map/backward/pallas_call | solution.py:125
  63.3 0.0 collective-permute-done.10
  63.3 0.0 collective-permute-done.11
  63.3 3.9 %backward.5 = (bf16[256,256]{1,0:T(8,128)(2,1)S(1)}, bf16[256,256]{1,0:T(8,128)(2,1)S(1)}, bf16[2048,384]{1,0:T(8,128)(2,1)}) custom-call(s32[1]{0:T(128)} %bitcast.1.z_ref, bf16[256,256]{1,0:T(8,128)(2,1)S(1)} %pad_maximum_fusion.1.refs_0_, bf16[256,256]{1,0:T(8,128)(2,1)S(1)} %collective-permute-done.4.refs_1_, f32[128,512]{1,0:T(8,128)S(1)} %get-tuple-element.49.refs_2_, ...), custom_call_target="tpu_custom_call" | custom-call | tf_op jit(solution)/shard_map/backward/pallas_call | solution.py:125
  67.2 5.8 %all-to-all-start.2 = ((bf16[16,128,384]{2,1,0:T(8,128)(2,1)}), bf16[16,128,384]{2,1,0:T(8,128)(2,1)}, u32[]{:S(2)}, u32[]{:S(2)}) async-start(bf16[16,128,384]{2,1,0:T(8,128)(2,1)} %bitcast.12), calls=%async_computation.2 | async-start | bytes 3145728 | tf_op jit(solution)/shard_map/all_to_all | solution.py:175
  73.0 1.6 %collective-permute-start.12 = (bf16[256,256]{1,0:T(8,128)(2,1)S(1)}, bf16[256,256]{1,0:T(8,128)(2,1)S(1)}, u32[]{:S(2)}, u32[]{:S(2)}) collective-permute-start(bf16[256,256]{1,0:T(8,128)(2,1)S(1)} %add_convert_fusion.5), channel_id=1, source_target_pairs={{0,14},{2,0},{4,2},{6,4},{8,6},{10,8},{12,10},{14,12},{1,15},{3,1}... | collective-permute-start | bytes 393224 | tf_op jit(solution)/shard_map/ppermute | solution.py:165
  74.6 0.1 collective-permute-start.15
  74.7 2.2 %collective-permute-done.12 = bf16[256,256]{1,0:T(8,128)(2,1)S(1)} collective-permute-done((bf16[256,256]{1,0:T(8,128)(2,1)S(1)}, bf16[256,256]{1,0:T(8,128)(2,1)S(1)}, u32[]{:S(2)}, u32[]{:S(2)}) %collective-permute-start.12) | collective-permute-done | bytes 131104 | tf_op jit(solution)/shard_map/ppermute | solution.py:165
  76.9 2.8 %collective-permute-start.13 = (bf16[256,256]{1,0:T(8,128)(2,1)S(1)}, bf16[256,256]{1,0:T(8,128)(2,1)S(1)}, u32[]{:S(2)}, u32[]{:S(2)}) collective-permute-start(bf16[256,256]{1,0:T(8,128)(2,1)S(1)} %add_convert_fusion.4), channel_id=1, source_target_pairs={{0,14},{2,0},{4,2},{6,4},{8,6},{10,8},{12,10},{14,12},{1,15},{3,1}... | collective-permute-start | bytes 393224 | tf_op jit(solution)/shard_map/ppermute | solution.py:165
  79.7 0.0 collective-permute-done.15
  79.8 0.1 collective-permute-start.16
  79.9 1.8 %collective-permute-done.13 = bf16[256,256]{1,0:T(8,128)(2,1)S(1)} collective-permute-done((bf16[256,256]{1,0:T(8,128)(2,1)S(1)}, bf16[256,256]{1,0:T(8,128)(2,1)S(1)}, u32[]{:S(2)}, u32[]{:S(2)}) %collective-permute-start.13) | collective-permute-done | bytes 131104 | tf_op jit(solution)/shard_map/ppermute | solution.py:165
  81.7 3.2 %collective-permute-start.14 = (bf16[128,256]{1,0:T(8,128)(2,1)S(1)}, bf16[128,256]{1,0:T(8,128)(2,1)S(1)}, u32[]{:S(2)}, u32[]{:S(2)}) collective-permute-start(bf16[128,256]{1,0:T(8,128)(2,1)S(1)} %get-tuple-element.60), channel_id=1, source_target_pairs={{0,14},{2,0},{4,2},{6,4},{8,6},{10,8},{12,10},{14,12},{1,15},{3,1}... | collective-permute-start | bytes 196616 | tf_op jit(solution)/shard_map/ppermute | solution.py:165
  84.9 1.1 %collective-permute-start.17 = (bf16[128,256]{1,0:T(8,128)(2,1)S(1)}, bf16[128,256]{1,0:T(8,128)(2,1)S(1)}, u32[]{:S(2)}, u32[]{:S(2)}) collective-permute-start(bf16[128,256]{1,0:T(8,128)(2,1)S(1)} %get-tuple-element.61), channel_id=1, source_target_pairs={{0,15},{1,14},{2,1},{3,0},{4,3},{5,2},{6,5},{7,4},{8,7},{9,6},{10,... | collective-permute-start | bytes 196616 | tf_op jit(solution)/shard_map/ppermute | solution.py:171
  86.0 0.0 collective-permute-done.16
  86.1 0.5 collective-permute-start.18
  86.6 0.0 collective-permute-done.14
  86.6 3.3 %collective-permute-done.17 = bf16[128,256]{1,0:T(8,128)(2,1)S(1)} collective-permute-done((bf16[128,256]{1,0:T(8,128)(2,1)S(1)}, bf16[128,256]{1,0:T(8,128)(2,1)S(1)}, u32[]{:S(2)}, u32[]{:S(2)}) %collective-permute-start.17) | collective-permute-done | bytes 65568 | tf_op jit(solution)/shard_map/ppermute | solution.py:171
  89.9 2.4 %collective-permute-done.18 = bf16[128,256]{1,0:T(8,128)(2,1)S(1)} collective-permute-done((bf16[128,256]{1,0:T(8,128)(2,1)S(1)}, bf16[128,256]{1,0:T(8,128)(2,1)S(1)}, u32[]{:S(2)}, u32[]{:S(2)}) %collective-permute-start.18) | collective-permute-done | bytes 65568 | tf_op jit(solution)/shard_map/ppermute | solution.py:160
  92.5 0.0 all-to-all-done.2
  92.5 1.7 %convert_reduce_fusion = f32[2,128,384]{2,1,0:T(8,128)S(1)} fusion(bf16[8,2,128,384]{3,2,1,0:T(8,128)(2,1)} %bitcast.19), kind=kLoop, calls=%fused_computation.2 | loop fusion | flops 1474560 | bytes 1966080 | tf_op jit(solution)/shard_map/reduce_sum | solution.py:243
  94.3 8.0 %collective-permute-start.19 = (bf16[64,1024]{1,0:T(8,128)(2,1)S(1)}, bf16[64,1024]{1,0:T(8,128)(2,1)S(1)}, u32[]{:S(2)}, u32[]{:S(2)}) collective-permute-start(bf16[64,1024]{1,0:T(8,128)(2,1)S(1)} %get-tuple-element.58), channel_id=1, source_target_pairs={{0,64},{64,0},{1,65},{65,1},{2,66},{66,2},{3,67},{67,3},{4,68},{68... | collective-permute-start | bytes 393224 | tf_op jit(solution)/shard_map/ppermute | solution.py:160
  102.3 1.0 collective-permute-done.19.away_ref
  103.3 0.7 join_heads.1
  (41 shorter events, 0.7 us)
Async XLA Ops:
  1.5 4.2 %collective-permute-start = (bf16[64,512]{1,0:T(8,128)(2,1)S(1)}, bf16[64,512]{1,0:T(8,128)(2,1)S(1)}, u32[]{:S(2)}, u32[]{:S(2)}) collective-permute-start(bf16[64,512]{1,0:T(8,128)(2,1)S(1)} %pad_maximum_fusion.4), channel_id=1, source_target_pairs={{0,64},{64,0},{1,65},{65,1},{2,66},{66,2},{3,67},{67,3},{4,68},{68... | collective-permute-start | bytes 196616 | tf_op jit(solution)/shard_map/ppermute | solution.py:160
  5.7 1.3 %collective-permute-start.7 = (bf16[64,512]{1,0:T(8,128)(2,1)S(1)}, bf16[64,512]{1,0:T(8,128)(2,1)S(1)}, u32[]{:S(2)}, u32[]{:S(2)}) collective-permute-start(bf16[64,512]{1,0:T(8,128)(2,1)S(1)} %pad_maximum_fusion.6), channel_id=1, source_target_pairs={{0,64},{64,0},{1,65},{65,1},{2,66},{66,2},{3,67},{67,3},{4,68},{68... | collective-permute-start | bytes 196616 | tf_op jit(solution)/shard_map/ppermute | solution.py:160
  6.2 7.3 %collective-permute-start.1 = (bf16[128,256]{1,0:T(8,128)(2,1)S(1)}, bf16[128,256]{1,0:T(8,128)(2,1)S(1)}, u32[]{:S(2)}, u32[]{:S(2)}) collective-permute-start(bf16[128,256]{1,0:T(8,128)(2,1)S(1)} %pad_maximum_fusion.5), channel_id=1, source_target_pairs={{0,1},{1,0},{2,3},{3,2},{4,5},{5,4},{6,7},{7,6},{8,9},{9,8},{10,11... | collective-permute-start | bytes 196616 | tf_op jit(solution)/shard_map/ppermute | solution.py:160
  7.1 15.3 %copy-start = (s32[8]{0:T(128)S(1)}, s32[8]{0:T(128)}, u32[]{:S(2)}) copy-start(s32[8]{0:T(128)} %constant.72) | copy-start | bytes 100
  8.3 24.6 %all-to-all-start = ((bf16[16,128,256]{2,1,0:T(8,128)(2,1)}), bf16[16,128,256]{2,1,0:T(8,128)(2,1)S(1)}, u32[]{:S(2)}, u32[]{:S(2)}) async-start(bf16[16,128,256]{2,1,0:T(8,128)(2,1)} %bitcast.4), calls=%async_computation | async-start | bytes 2097152 | tf_op jit(solution)/shard_map/all_to_all | solution.py:175
  13.6 8.8 %collective-permute-start.4 = (bf16[256,256]{1,0:T(8,128)(2,1)S(1)}, bf16[256,256]{1,0:T(8,128)(2,1)S(1)}, u32[]{:S(2)}, u32[]{:S(2)}) collective-permute-start(bf16[256,256]{1,0:T(8,128)(2,1)S(1)} %pad_maximum_fusion.1.refs_0_), channel_id=1, source_target_pairs={{0,2},{2,4},{4,6},{6,8},{8,10},{10,12},{12,14},{14,0},{1,3},{3,5},... | collective-permute-start | bytes 393224 | tf_op jit(solution)/shard_map/ppermute | solution.py:165
  15.3 7.8 %collective-permute-start.2 = (bf16[256,256]{1,0:T(8,128)(2,1)S(1)}, bf16[256,256]{1,0:T(8,128)(2,1)S(1)}, u32[]{:S(2)}, u32[]{:S(2)}) collective-permute-start(bf16[256,256]{1,0:T(8,128)(2,1)S(1)} %pad_maximum_fusion.1.refs_0_), channel_id=1, source_target_pairs={{0,14},{2,0},{4,2},{6,4},{8,6},{10,8},{12,10},{14,12},{1,15},{3,1}... | collective-permute-start | bytes 393224 | tf_op jit(solution)/shard_map/ppermute | solution.py:165
  22.4 5.3 %collective-permute-start.5 = (bf16[256,256]{1,0:T(8,128)(2,1)S(1)}, bf16[256,256]{1,0:T(8,128)(2,1)S(1)}, u32[]{:S(2)}, u32[]{:S(2)}) collective-permute-start(bf16[256,256]{1,0:T(8,128)(2,1)S(1)} %collective-permute-done.4.refs_1_), channel_id=1, source_target_pairs={{0,2},{2,4},{4,6},{6,8},{8,10},{10,12},{12,14},{14,0},{1,3},{3,5},... | collective-permute-start | bytes 393224 | tf_op jit(solution)/shard_map/ppermute | solution.py:165
  23.1 4.7 %collective-permute-start.3 = (bf16[256,256]{1,0:T(8,128)(2,1)S(1)}, bf16[256,256]{1,0:T(8,128)(2,1)S(1)}, u32[]{:S(2)}, u32[]{:S(2)}) collective-permute-start(bf16[256,256]{1,0:T(8,128)(2,1)S(1)} %collective-permute-done.2.refs_2_), channel_id=1, source_target_pairs={{0,14},{2,0},{4,2},{6,4},{8,6},{10,8},{12,10},{14,12},{1,15},{3,1}... | collective-permute-start | bytes 393224 | tf_op jit(solution)/shard_map/ppermute | solution.py:165
  27.7 5.0 %collective-permute-start.6 = (bf16[256,256]{1,0:T(8,128)(2,1)S(1)}, bf16[256,256]{1,0:T(8,128)(2,1)S(1)}, u32[]{:S(2)}, u32[]{:S(2)}) collective-permute-start(bf16[256,256]{1,0:T(8,128)(2,1)S(1)} %collective-permute-done.5.refs_3_), channel_id=1, source_target_pairs={{0,2},{2,4},{4,6},{6,8},{8,10},{10,12},{12,14},{14,0},{1,3},{3,5},... | collective-permute-start | bytes 393224 | tf_op jit(solution)/shard_map/ppermute | solution.py:165
  27.8 9.9 %collective-permute-start.8 = (bf16[256,256]{1,0:T(8,128)(2,1)S(1)}, bf16[256,256]{1,0:T(8,128)(2,1)S(1)}, u32[]{:S(2)}, u32[]{:S(2)}) collective-permute-start(bf16[256,256]{1,0:T(8,128)(2,1)S(1)} %collective-permute-done.3.refs_0_), channel_id=1, source_target_pairs={{0,14},{2,0},{4,2},{6,4},{8,6},{10,8},{12,10},{14,12},{1,15},{3,1}... | collective-permute-start | bytes 393224 | tf_op jit(solution)/shard_map/ppermute | solution.py:165
  32.7 5.0 %collective-permute-start.9 = (bf16[256,256]{1,0:T(8,128)(2,1)S(1)}, bf16[256,256]{1,0:T(8,128)(2,1)S(1)}, u32[]{:S(2)}, u32[]{:S(2)}) collective-permute-start(bf16[256,256]{1,0:T(8,128)(2,1)S(1)} %collective-permute-done.6.refs_1_), channel_id=1, source_target_pairs={{0,2},{2,4},{4,6},{6,8},{8,10},{10,12},{12,14},{14,0},{1,3},{3,5},... | collective-permute-start | bytes 393224 | tf_op jit(solution)/shard_map/ppermute | solution.py:165
  56.4 6.9 %collective-permute-start.10 = (bf16[256,256]{1,0:T(8,128)(2,1)S(1)}, bf16[256,256]{1,0:T(8,128)(2,1)S(1)}, u32[]{:S(2)}, u32[]{:S(2)}) collective-permute-start(bf16[256,256]{1,0:T(8,128)(2,1)S(1)} %get-tuple-element.44), channel_id=1, source_target_pairs={{0,14},{2,0},{4,2},{6,4},{8,6},{10,8},{12,10},{14,12},{1,15},{3,1}... | collective-permute-start | bytes 393224 | tf_op jit(solution)/shard_map/ppermute | solution.py:165
  56.5 6.8 %collective-permute-start.11 = (bf16[256,256]{1,0:T(8,128)(2,1)S(1)}, bf16[256,256]{1,0:T(8,128)(2,1)S(1)}, u32[]{:S(2)}, u32[]{:S(2)}) collective-permute-start(bf16[256,256]{1,0:T(8,128)(2,1)S(1)} %get-tuple-element.45), channel_id=1, source_target_pairs={{0,2},{2,4},{4,6},{6,8},{8,10},{10,12},{12,14},{14,0},{1,3},{3,5},... | collective-permute-start | bytes 393224 | tf_op jit(solution)/shard_map/ppermute | solution.py:165
  67.2 25.3 %all-to-all-start.2 = ((bf16[16,128,384]{2,1,0:T(8,128)(2,1)}), bf16[16,128,384]{2,1,0:T(8,128)(2,1)}, u32[]{:S(2)}, u32[]{:S(2)}) async-start(bf16[16,128,384]{2,1,0:T(8,128)(2,1)} %bitcast.12), calls=%async_computation.2 | async-start | bytes 3145728 | tf_op jit(solution)/shard_map/all_to_all | solution.py:175
  73.0 3.9 %collective-permute-start.12 = (bf16[256,256]{1,0:T(8,128)(2,1)S(1)}, bf16[256,256]{1,0:T(8,128)(2,1)S(1)}, u32[]{:S(2)}, u32[]{:S(2)}) collective-permute-start(bf16[256,256]{1,0:T(8,128)(2,1)S(1)} %add_convert_fusion.5), channel_id=1, source_target_pairs={{0,14},{2,0},{4,2},{6,4},{8,6},{10,8},{12,10},{14,12},{1,15},{3,1}... | collective-permute-start | bytes 393224 | tf_op jit(solution)/shard_map/ppermute | solution.py:165
  74.6 5.1 %collective-permute-start.15 = (bf16[256,256]{1,0:T(8,128)(2,1)S(1)}, bf16[256,256]{1,0:T(8,128)(2,1)S(1)}, u32[]{:S(2)}, u32[]{:S(2)}) collective-permute-start(bf16[256,256]{1,0:T(8,128)(2,1)S(1)} %add_convert_fusion.2), channel_id=1, source_target_pairs={{0,2},{2,4},{4,6},{6,8},{8,10},{10,12},{12,14},{14,0},{1,3},{3,5},... | collective-permute-start | bytes 393224 | tf_op jit(solution)/shard_map/ppermute | solution.py:165
  76.9 4.8 %collective-permute-start.13 = (bf16[256,256]{1,0:T(8,128)(2,1)S(1)}, bf16[256,256]{1,0:T(8,128)(2,1)S(1)}, u32[]{:S(2)}, u32[]{:S(2)}) collective-permute-start(bf16[256,256]{1,0:T(8,128)(2,1)S(1)} %add_convert_fusion.4), channel_id=1, source_target_pairs={{0,14},{2,0},{4,2},{6,4},{8,6},{10,8},{12,10},{14,12},{1,15},{3,1}... | collective-permute-start | bytes 393224 | tf_op jit(solution)/shard_map/ppermute | solution.py:165
  79.8 6.2 %collective-permute-start.16 = (bf16[256,256]{1,0:T(8,128)(2,1)S(1)}, bf16[256,256]{1,0:T(8,128)(2,1)S(1)}, u32[]{:S(2)}, u32[]{:S(2)}) collective-permute-start(bf16[256,256]{1,0:T(8,128)(2,1)S(1)} %add_convert_fusion.1), channel_id=1, source_target_pairs={{0,2},{2,4},{4,6},{6,8},{8,10},{10,12},{12,14},{14,0},{1,3},{3,5},... | collective-permute-start | bytes 393224 | tf_op jit(solution)/shard_map/ppermute | solution.py:165
  81.7 4.8 %collective-permute-start.14 = (bf16[128,256]{1,0:T(8,128)(2,1)S(1)}, bf16[128,256]{1,0:T(8,128)(2,1)S(1)}, u32[]{:S(2)}, u32[]{:S(2)}) collective-permute-start(bf16[128,256]{1,0:T(8,128)(2,1)S(1)} %get-tuple-element.60), channel_id=1, source_target_pairs={{0,14},{2,0},{4,2},{6,4},{8,6},{10,8},{12,10},{14,12},{1,15},{3,1}... | collective-permute-start | bytes 196616 | tf_op jit(solution)/shard_map/ppermute | solution.py:165
  84.9 5.0 %collective-permute-start.17 = (bf16[128,256]{1,0:T(8,128)(2,1)S(1)}, bf16[128,256]{1,0:T(8,128)(2,1)S(1)}, u32[]{:S(2)}, u32[]{:S(2)}) collective-permute-start(bf16[128,256]{1,0:T(8,128)(2,1)S(1)} %get-tuple-element.61), channel_id=1, source_target_pairs={{0,15},{1,14},{2,1},{3,0},{4,3},{5,2},{6,5},{7,4},{8,7},{9,6},{10,... | collective-permute-start | bytes 196616 | tf_op jit(solution)/shard_map/ppermute | solution.py:171
  86.1 6.3 %collective-permute-start.18 = (bf16[128,256]{1,0:T(8,128)(2,1)S(1)}, bf16[128,256]{1,0:T(8,128)(2,1)S(1)}, u32[]{:S(2)}, u32[]{:S(2)}) collective-permute-start(bf16[128,256]{1,0:T(8,128)(2,1)S(1)} %slice.158), channel_id=1, source_target_pairs={{0,1},{1,0},{2,3},{3,2},{4,5},{5,4},{6,7},{7,6},{8,9},{9,8},{10,11... | collective-permute-start | bytes 196616 | tf_op jit(solution)/shard_map/ppermute | solution.py:160
  94.3 9.0 %collective-permute-start.19 = (bf16[64,1024]{1,0:T(8,128)(2,1)S(1)}, bf16[64,1024]{1,0:T(8,128)(2,1)S(1)}, u32[]{:S(2)}, u32[]{:S(2)}) collective-permute-start(bf16[64,1024]{1,0:T(8,128)(2,1)S(1)} %get-tuple-element.58), channel_id=1, source_target_pairs={{0,64},{64,0},{1,65},{65,1},{2,66},{66,2},{3,67},{67,3},{4,68},{68... | collective-permute-start | bytes 393224 | tf_op jit(solution)/shard_map/ppermute | solution.py:160
